TPU v7x, 512 devices: a whole 4x8x8 slice. The times are simulated.
512 devices in a mesh: ctx: 128 (over z, y, core), tile: 4 (over x).
Axes of the slice: x: 4, y: 8, z: 8, core: 2. Of those that a mesh axis runs over, the one named last changes fastest.
Arguments:
- masks: bfloat16 [256, 512, 512], P('ctx', 'tile'), may hold values from 0 to 1
- blur_rows: bfloat16 [512, 512], replicated, may hold values from -0.25 to 0.25
- blur_cols: bfloat16 [512, 512], replicated, may hold values from -0.25 to 0.25
- pupils: float32 [6, 64, 128], replicated, may hold values from -5 to 5
- targets: bfloat16 [256, 512, 512], P('ctx', 'tile'), may hold values from 0 to 1
- context_masters: int32 [256, 12], P('ctx'), may hold values from 0 to 255, as said below
- offsets: int32 [256, 12, 2], P('ctx'), may hold values from 0 to 511
Outputs:
- resist: bfloat16 [256, 512, 512], P('ctx', 'tile')
- mask_grad: float32 [256, 512, 512], P('ctx', 'tile')
Inputs may be any that keep to these rules, and one draw needn't show every extreme that they name: `context_masters`: master m lies on ctx index m // 2. Among the masters named by the 2 contexts of one ctx index there is at most one lying on any one ctx index; a master may be named several times.
All inputs are finite; a program needn't handle non-finite values.
Results may differ from a plain program's by a relative error of at most 0.019.
Values may be sent and summed in bfloat16 or wider, within the bound.
A program may use at most 64 MiB of HBM per device.

v0:
```python
import math

import jax
import jax.numpy as jnp
from jax import lax
from jax.sharding import PartitionSpec as P

STEEPNESS = 4.0
THRESHOLD = 1.0


def joined_along(blocks, dim):
    dims = list(blocks.shape[1:])
    dims[dim] *= blocks.shape[0]
    return jnp.moveaxis(blocks, 0, dim).reshape(dims)


def copy_for_each(array, axis):
    devices = lax.axis_size(axis)
    return lax.all_to_all(
        jnp.broadcast_to(array[None], (devices, *array.shape)), axis, 0, 0, tiled=True
    )


def collect(array, axis, dim):
    return joined_along(copy_for_each(array, axis), dim)


def split_up(array, dim, devices):
    dims = array.shape
    blocks = array.reshape(*dims[:dim], devices, dims[dim] // devices, *dims[dim + 1 :])
    return jnp.moveaxis(blocks, dim, 0)


def summed_on_arrival(array, axis, dim):
    devices = lax.axis_size(axis)
    blocks = lax.all_to_all(split_up(array, dim, devices), axis, 0, 0, tiled=True)
    return jnp.sum(blocks.astype(jnp.float32), axis=0)


def build_tables(extent, mode_count):
    frequency = (jnp.arange(mode_count, dtype=jnp.int32) - mode_count // 2) % extent
    positions = jnp.arange(extent, dtype=jnp.int32)
    windings = frequency[:, None] * positions[None, :] % extent
    angles = windings.astype(jnp.float32) * (2.0 * math.pi / extent)
    scale_factor = 1.0 / math.sqrt(extent)
    cosine_table = jnp.cos(angles) * scale_factor
    sine_table = jnp.sin(angles) * scale_factor
    row_real = cosine_table.astype(jnp.bfloat16)
    row_imag = (-sine_table).astype(jnp.bfloat16)
    col_fwd = jnp.concatenate([cosine_table.T, -sine_table.T], axis=1).astype(jnp.bfloat16)
    inverse_big = jnp.concatenate(
        [
            jnp.concatenate([cosine_table, sine_table], axis=1),
            jnp.concatenate([-sine_table, cosine_table], axis=1),
        ],
        axis=0,
    ).astype(jnp.bfloat16)
    back_real = cosine_table.T.astype(jnp.bfloat16)
    back_imag = sine_table.T.astype(jnp.bfloat16)
    adjoint_big = jnp.concatenate(
        [
            jnp.concatenate([cosine_table.T, -sine_table.T], axis=1),
            jnp.concatenate([sine_table.T, cosine_table.T], axis=1),
        ],
        axis=0,
    ).astype(jnp.bfloat16)
    return (row_real, row_imag, col_fwd, inverse_big, back_real, back_imag, adjoint_big)


def complex_left(left_real, left_imag, values):
    width = values.shape[-1] // 2
    real_lead = jnp.einsum("ux,...xv->...uv", left_real, values, preferred_element_type=jnp.float32)
    imag_lead = jnp.einsum("ux,...xv->...uv", left_imag, values, preferred_element_type=jnp.float32)
    return jnp.concatenate(
        [
            real_lead[..., :width] - imag_lead[..., width:],
            real_lead[..., width:] + imag_lead[..., :width],
        ],
        axis=-1,
    )


def complex_times(factor, values, conjugate):
    width = values.shape[-1] // 2
    factor_real = factor[..., :width]
    factor_imag = factor[..., width:]
    if conjugate:
        factor_imag = -factor_imag
    values_real = values[..., :width]
    values_imag = values[..., width:]
    return jnp.concatenate(
        [
            factor_real * values_real - factor_imag * values_imag,
            factor_real * values_imag + factor_imag * values_real,
        ],
        axis=-1,
    )


def phase_table(shifts, row_begin, band_rows, mode_count, extent):
    freq_u = (jnp.arange(band_rows, dtype=jnp.int32) + row_begin - mode_count // 2) % extent
    freq_v = (jnp.arange(mode_count, dtype=jnp.int32) - mode_count // 2) % extent
    windings = (
        freq_u[None, :, None] * shifts[:, 0][:, None, None]
        + freq_v[None, None, :] * shifts[:, 1][:, None, None]
    ) % extent
    angles = windings.astype(jnp.float32) * (2.0 * math.pi / extent)
    return jnp.concatenate([jnp.cos(angles), -jnp.sin(angles)], axis=-1)


def image_adjoint(
    spectrum, target, pupils, back_real, back_imag, row_real, row_imag, inverse_big, adjoint_big
):
    amplitude = complex_times(pupils, spectrum[None], False).astype(jnp.bfloat16)
    spread = jnp.einsum(
        "kuv,vy->kuy", amplitude, inverse_big, preferred_element_type=jnp.float32
    ).astype(jnp.bfloat16)
    field = complex_left(back_real, back_imag, spread)
    width = field.shape[-1] // 2
    field_real = field[..., :width]
    field_imag = field[..., width:]
    intensity = jnp.sum(field_real * field_real + field_imag * field_imag, axis=0)
    resist = jax.nn.sigmoid(STEEPNESS * (intensity - THRESHOLD))
    slope_term = (resist - target.astype(jnp.float32)) * STEEPNESS * resist * (1.0 - resist)
    pull_back = jnp.concatenate(
        [2.0 * slope_term * field_real, 2.0 * slope_term * field_imag], axis=-1
    ).astype(jnp.bfloat16)
    folded = jnp.einsum(
        "kxy,yv->kxv", pull_back, adjoint_big, preferred_element_type=jnp.float32
    ).astype(jnp.bfloat16)
    grad_amp = complex_left(row_real, row_imag, folded)
    grad_spec = jnp.sum(complex_times(pupils, grad_amp, True), axis=0)
    return (resist.astype(jnp.bfloat16), grad_spec)


def local(masks, blur_rows, blur_cols, pupils, targets, context_masters, offsets):
    ctx_count = lax.axis_size("ctx")
    tile_count = lax.axis_size("tile")
    owned, row_count, extent = masks.shape
    mode_count = pupils.shape[1]
    context_count = context_masters.shape[0]
    source_count = context_masters.shape[1]
    tile_pos = lax.axis_index("tile")
    row_start = tile_pos * row_count
    row_real, row_imag, col_fwd, inverse_big, back_real, back_imag, adjoint_big = build_tables(
        extent, mode_count
    )
    own_row_real = lax.dynamic_slice_in_dim(row_real, row_start, row_count, 1)
    own_row_imag = lax.dynamic_slice_in_dim(row_imag, row_start, row_count, 1)
    own_back_real = lax.dynamic_slice_in_dim(back_real, row_start, row_count, 0)
    own_back_imag = lax.dynamic_slice_in_dim(back_imag, row_start, row_count, 0)
    own_blur = lax.dynamic_slice_in_dim(blur_rows, row_start, row_count, 0)
    owners = (context_masters // owned).reshape(-1)
    local_index = (context_masters % owned).reshape(-1)
    slot_index = jnp.arange(ctx_count, dtype=jnp.int32)
    owner_match = owners[:, None] == slot_index[None, :]
    wanted = jnp.max(jnp.where(owner_match, local_index[:, None] + 1, 0), axis=0)
    asked_for = lax.all_to_all(wanted[:, None], "ctx", split_axis=0, concat_axis=0, tiled=True)[
        :, 0
    ]
    chosen = asked_for[:, None] == jnp.arange(owned, dtype=jnp.int32)[None, :] + 1
    half_blur = jnp.einsum(
        "mxy,zy->mxz", masks, blur_cols, preferred_element_type=jnp.float32
    ).astype(jnp.bfloat16)
    weights = own_blur
    blurred = jnp.einsum(
        "xj,mjz->mxz", weights, collect(half_blur, "tile", 1), preferred_element_type=jnp.float32
    ).astype(jnp.bfloat16)
    column = jnp.einsum("mxy,yv->mxv", blurred, col_fwd, preferred_element_type=jnp.float32).astype(
        jnp.bfloat16
    )
    partial_value = complex_left(own_row_real, own_row_imag, column)
    quarter = mode_count // tile_count
    spectra = summed_on_arrival(partial_value.astype(jnp.bfloat16), "tile", 1).astype(jnp.bfloat16)
    outgoing = jnp.einsum(
        "dm,muv->duv", chosen.astype(jnp.bfloat16), spectra, preferred_element_type=jnp.float32
    ).astype(jnp.bfloat16)
    incoming = lax.all_to_all(outgoing, "ctx", split_axis=0, concat_axis=0, tiled=True)
    incoming = collect(incoming, "tile", 1)
    flat_shift = offsets.reshape(-1, 2)
    picked = jnp.take(incoming, owners, axis=0).astype(jnp.float32)
    turned = complex_times(
        phase_table(flat_shift, 0, mode_count, mode_count, extent), picked, False
    )
    context_spec = jnp.sum(
        turned.reshape(context_count, source_count, mode_count, 2 * mode_count), axis=1
    )

    def one_context(inputs):
        spectrum, target = inputs
        return image_adjoint(
            spectrum,
            target,
            pupils,
            own_back_real,
            own_back_imag,
            own_row_real,
            own_row_imag,
            inverse_big,
            adjoint_big,
        )

    resist, grad_part = lax.map(one_context, (context_spec, targets))
    grad_ctx = summed_on_arrival(grad_part.astype(jnp.bfloat16), "tile", 1)
    band_start = tile_pos * quarter
    repeated = jnp.repeat(grad_ctx, source_count, axis=0)
    back_turn = complex_times(
        phase_table(flat_shift, band_start, quarter, mode_count, extent), repeated, True
    )
    returned = jnp.einsum(
        "rd,ruv->duv", owner_match.astype(jnp.float32), back_turn, precision=lax.Precision.HIGHEST
    )
    arrived = lax.all_to_all(
        returned.astype(jnp.bfloat16), "ctx", split_axis=0, concat_axis=0, tiled=True
    ).astype(returned.dtype)
    master_grad = jnp.einsum(
        "dm,duv->muv", chosen.astype(jnp.float32), arrived, precision=lax.Precision.HIGHEST
    ).astype(jnp.bfloat16)
    master_grad = collect(master_grad, "tile", 1)
    lifted = jnp.einsum(
        "muv,vy->muy", master_grad, inverse_big, preferred_element_type=jnp.float32
    ).astype(jnp.bfloat16)
    surface = (
        jnp.einsum(
            "xu,muy->mxy", own_back_real, lifted[..., :extent], preferred_element_type=jnp.float32
        )
        - jnp.einsum(
            "xu,muy->mxy", own_back_imag, lifted[..., extent:], preferred_element_type=jnp.float32
        )
    ).astype(jnp.bfloat16)
    settled = jnp.einsum(
        "mxy,yz->mxz", surface, blur_cols, preferred_element_type=jnp.float32
    ).astype(jnp.bfloat16)
    weights = own_blur
    mask_grad = jnp.transpose(
        summed_on_arrival(
            jnp.einsum("xj,mxz->jmz", weights, settled, preferred_element_type=jnp.float32).astype(
                jnp.bfloat16
            ),
            "tile",
            0,
        ),
        (1, 0, 2),
    )
    return (resist, mask_grad)


def solution(mesh):
    placed = (
        P("ctx", "tile", None),
        P(),
        P(),
        P(),
        P("ctx", "tile", None),
        P("ctx", None),
        P("ctx", None, None),
    )
    return jax.shard_map(
        local,
        mesh=mesh,
        in_specs=placed,
        out_specs=(P("ctx", "tile", None), P("ctx", "tile", None)),
        check_vma=False,
    )
```

profile of v0, /device:TPU:1, one launch (start us, length us, event | category | flops | bytes accessed | tf_op | source)
XLA Modules:
  0.0 216.2 jit_solution(15076062880644929669)
XLA Ops:
  0.6 1.5 convolution_convert_fusion.7
  3.3 4.8 %all-to-all-start.1 = ((bf16[4,2,128,512]{3,2,1,0:T(8,128)(2,1)}), bf16[4,2,128,512]{3,2,1,0:T(8,128)(2,1)S(1)}, u32[]{:S(2)}, u32[]{:S(2)}) async-start(bf16[4,2,128,512]{3,2,1,0:T(8,128)(2,1)} %broadcast_in_dim.75), calls=%async_computation.1 | async-start | bytes 2097152 | tf_op jit(solution)/shard_map/all_to_all | solution.py:20
  11.0 6.8 %all-to-all-done.1 = bf16[4,2,128,512]{3,2,1,0:T(8,128)(2,1)S(1)} async-done(((bf16[4,2,128,512]{3,2,1,0:T(8,128)(2,1)}), bf16[4,2,128,512]{3,2,1,0:T(8,128)(2,1)S(1)}, u32[]{:S(2)}, u32[]{:S(2)}) %all-to-all-start.1) | async-done | bytes 1048608 | tf_op jit(solution)/shard_map/all_to_all | solution.py:20
  17.8 23.2 %all-to-all-start = ((s32[128,1,1]{2,1,0:T(1,128)}), s32[128,1,1]{2,1,0:T(1,128)S(1)}, u32[]{:S(2)}, u32[]{:S(2)}) async-start(s32[128,1,1]{2,1,0:T(1,128)} %copy.54), calls=%async_computation | async-start | bytes 131072 | tf_op jit(solution)/shard_map/all_to_all | solution.py:159
  43.0 9.5 %all-to-all-done = s32[128,1,1]{2,1,0:T(1,128)S(1)} async-done(((s32[128,1,1]{2,1,0:T(1,128)}), s32[128,1,1]{2,1,0:T(1,128)S(1)}, u32[]{:S(2)}, u32[]{:S(2)}) %all-to-all-start) | async-done | bytes 544 | tf_op jit(solution)/shard_map/all_to_all | solution.py:159
  52.5 3.3 %all-to-all-start.2 = ((bf16[4,2,16,128]{3,2,1,0:T(8,128)(2,1)}), bf16[4,2,16,128]{3,2,1,0:T(8,128)(2,1)S(1)}, u32[]{:S(2)}, u32[]{:S(2)}) async-start(bf16[4,2,16,128]{3,2,1,0:T(8,128)(2,1)} %copy_bitcast_fusion), calls=%async_computation.2 | async-start | bytes 65536 | tf_op jit(solution)/shard_map/all_to_all | solution.py:37
  55.7 2.4 %reduce.1 = s32[128]{0:T(128)S(1)} reduce(s32[128,1,1]{2,1,0:T(1,128)S(1)} %all-to-all-done, s32[]{:T(128)} %constant.159.clone.1), dimensions={1,2}, to_apply=%all_to_all.31.reduce_sub_computation | reduce | bytes 1028 | tf_op jit(solution)/shard_map/all_to_all | solution.py:159
  58.1 1.9 all-to-all-done.2
  61.6 6.9 %all-to-all-start.3 = ((bf16[128,16,128]{2,1,0:T(8,128)(2,1)}), bf16[128,16,128]{2,1,0:T(8,128)(2,1)S(1)}, u32[]{:S(2)}, u32[]{:S(2)}) async-start(bf16[128,16,128]{2,1,0:T(8,128)(2,1)} %copy.62), calls=%async_computation.3 | async-start | bytes 1048576 | tf_op jit(solution)/shard_map/all_to_all | solution.py:179
  70.0 19.2 %all-to-all-done.3 = bf16[128,16,128]{2,1,0:T(8,128)(2,1)S(1)} async-done(((bf16[128,16,128]{2,1,0:T(8,128)(2,1)}), bf16[128,16,128]{2,1,0:T(8,128)(2,1)S(1)}, u32[]{:S(2)}, u32[]{:S(2)}) %all-to-all-start.3) | async-done | bytes 524320 | tf_op jit(solution)/shard_map/all_to_all | solution.py:179
  89.2 1.6 broadcast_in_dim.76
  90.7 4.8 %all-to-all-start.4 = ((bf16[4,128,16,128]{3,2,1,0:T(8,128)(2,1)}), bf16[4,128,16,128]{3,2,1,0:T(8,128)(2,1)}, u32[]{:S(2)}, u32[]{:S(2)}) async-start(bf16[4,128,16,128]{3,2,1,0:T(8,128)(2,1)} %broadcast_in_dim.76), calls=%async_computation.4 | async-start | bytes 4194304 | tf_op jit(solution)/shard_map/all_to_all | solution.py:20
  98.3 23.9 %all-to-all-done.4 = bf16[4,128,16,128]{3,2,1,0:T(8,128)(2,1)} async-done(((bf16[4,128,16,128]{3,2,1,0:T(8,128)(2,1)}), bf16[4,128,16,128]{3,2,1,0:T(8,128)(2,1)}, u32[]{:S(2)}, u32[]{:S(2)}) %all-to-all-start.4) | async-done | bytes 2097184 | tf_op jit(solution)/shard_map/all_to_all | solution.py:20
  122.2 2.2 %copy.63 = bf16[4,128,16,128]{3,2,0,1:T(8,128)(2,1)S(1)} copy(bf16[4,128,16,128]{3,2,1,0:T(8,128)(2,1)} %all-to-all-done.4) | data formatting | bytes 4194304 | tf_op jit(solution)/shard_map/all_to_all | solution.py:20
  124.5 1.4 gather_fusion
  127.0 4.4 %multiply_subtract_fusion.1 = (f32[24,64,64]{2,1,0:T(8,128)S(1)}, f32[24,64,64]{2,1,0:T(8,128)S(1)}) fusion(f32[24,64,128]{2,1,0:T(8,128)S(1)} %select_convert_fusion, s32[24,64]{1,0:T(8,128)S(1)} %get-tuple-element.274, s32[24,64]{1,0:T(8,128)} %get-tuple-element.273), kind=kLoop, calls=%fused_computation.75 | loop fusion | flops 2064384 | bytes 1585152 | tf_op jit(solution)/shard_map/sub | solution.py:94
  132.5 19.1 %while.14 = (s32[]{:T(128)}, bf16[2,128,512]{2,1,0:T(8,128)(2,1)S(1)}, bf16[2,64,128]{2,1,0:T(8,128)(2,1)S(1)}, f32[6,64,128]{2,1,0:T(8,128)S(1)}, f32[2,64,128]...) while((s32[]{:T(128)}, ...), condition=%wide.region_6.7_spmd, body=%wide.region_3.6_spmd.sunk | while | flops 538632192 | bytes 55263464 | solution.py:204
  137.6 3.2 %multiply_convert_fusion.4 = (bf16[6,128,512]{1,2,0:T(8,128)(2,1)S(1)}, bf16[6,128,512]{1,2,0:T(8,128)(2,1)S(1)}) fusion(f32[128,512]{0,1:T(8,128)S(1)} %fusion.134, f32[6,128,1024]{1,2,0:T(8,128)} %copy-done.1, f32[6,128,1024]{1,2,0:T(8,128)} %copy-done.2), kind=kLoop, calls=%fused_computation.10.clone.1 | loop fusion | flops 2359296 | bytes 8126464 | tf_op jit(solution)/shard_map/convert.1
  147.2 3.2 %multiply_convert_fusion.4 = (bf16[6,128,512]{1,2,0:T(8,128)(2,1)S(1)}, bf16[6,128,512]{1,2,0:T(8,128)(2,1)S(1)}) fusion(f32[128,512]{0,1:T(8,128)S(1)} %fusion.134, f32[6,128,1024]{1,2,0:T(8,128)} %copy-done.1, f32[6,128,1024]{1,2,0:T(8,128)} %copy-done.2), kind=kLoop, calls=%fused_computation.10.clone.1 | loop fusion | flops 2359296 | bytes 8126464 | tf_op jit(solution)/shard_map/convert.1
  152.4 3.3 %all-to-all-start.5 = ((bf16[4,2,16,128]{3,2,1,0:T(8,128)(2,1)}), bf16[4,2,16,128]{3,2,1,0:T(8,128)(2,1)S(1)}, u32[]{:S(2)}, u32[]{:S(2)}) async-start(bf16[4,2,16,128]{3,2,1,0:T(8,128)(2,1)} %copy.67), calls=%async_computation.5 | async-start | bytes 65536 | tf_op jit(solution)/shard_map/all_to_all | solution.py:37
  155.7 4.2 %all-to-all-done.5 = bf16[4,2,16,128]{3,2,1,0:T(8,128)(2,1)S(1)} async-done(((bf16[4,2,16,128]{3,2,1,0:T(8,128)(2,1)}), bf16[4,2,16,128]{3,2,1,0:T(8,128)(2,1)S(1)}, u32[]{:S(2)}, u32[]{:S(2)}) %all-to-all-start.5) | async-done | bytes 32800 | tf_op jit(solution)/shard_map/all_to_all | solution.py:37
  162.1 26.9 %all_to_all.49 = bf16[128,16,128]{2,1,0:T(8,128)(2,1)S(1)} all-to-all(bf16[128,16,128]{2,1,0:T(8,128)(2,1)S(1)} %copy.70), channel_id=1, replica_groups=mesh['ctx'=128,'tile'=4] {'ctx'}, dimensions={0} | all-to-all | bytes 1048576 | tf_op jit(solution)/shard_map/all_to_all | solution.py:214
  189.3 7.1 %all_to_all.50 = bf16[4,2,16,128]{3,2,1,0:T(8,128)(2,1)S(1)} all-to-all(bf16[4,2,16,128]{3,2,1,0:T(8,128)(2,1)S(1)} %broadcast_in_dim.79), channel_id=1, replica_groups=mesh['ctx'=128,'tile'=4] {'tile'}, dimensions={0} | all-to-all | bytes 65536 | tf_op jit(solution)/shard_map/all_to_all | solution.py:20
  198.0 17.2 %all_to_all.51 = bf16[4,128,2,512]{3,1,2,0:T(8,128)(2,1)S(1)} all-to-all(bf16[4,128,2,512]{3,1,2,0:T(8,128)(2,1)S(1)} %copy.78), channel_id=1, replica_groups=mesh['ctx'=128,'tile'=4] {'tile'}, dimensions={0} | all-to-all | bytes 2097152 | tf_op jit(solution)/shard_map/all_to_all | solution.py:37
  (144 shorter events, 32.0 us)
Async XLA Ops:
  0.6 40.5 %copy-start = (bf16[512,512]{1,0:T(8,128)(2,1)S(1)}, bf16[512,512]{1,0:T(8,128)(2,1)}, u32[]{:S(2)}) copy-start(bf16[512,512]{1,0:T(8,128)(2,1)} %param.10) | copy-start | bytes 1572868
  2.2 5.9 %copy-start.17 = (s32[2,12]{1,0:T(2,128)S(1)}, s32[2,12]{1,0:T(2,128)}, u32[]{:S(2)}) copy-start(s32[2,12]{1,0:T(2,128)} %param.14) | copy-start | bytes 292
  3.3 14.6 %all-to-all-start.1 = ((bf16[4,2,128,512]{3,2,1,0:T(8,128)(2,1)}), bf16[4,2,128,512]{3,2,1,0:T(8,128)(2,1)S(1)}, u32[]{:S(2)}, u32[]{:S(2)}) async-start(bf16[4,2,128,512]{3,2,1,0:T(8,128)(2,1)} %broadcast_in_dim.75), calls=%async_computation.1 | async-start | bytes 2097152 | tf_op jit(solution)/shard_map/all_to_all | solution.py:20
  8.2 88.7 %copy-start.18 = (s32[24]{0:T(128)}, s32[24]{0:T(128)S(1)}, u32[]{:S(2)}) copy-start(s32[24]{0:T(128)S(1)} %reshape.304) | copy-start | bytes 292
  9.7 87.1 %copy-start.6 = (bf16[64,512]{1,0:T(8,128)(2,1)}, bf16[64,512]{1,0:T(8,128)(2,1)S(1)}, u32[]{:S(2)}) copy-start(bf16[64,512]{1,0:T(8,128)(2,1)S(1)} %get-tuple-element.270) | copy-start | bytes 196612
  17.8 34.6 %all-to-all-start = ((s32[128,1,1]{2,1,0:T(1,128)}), s32[128,1,1]{2,1,0:T(1,128)S(1)}, u32[]{:S(2)}, u32[]{:S(2)}) async-start(s32[128,1,1]{2,1,0:T(1,128)} %copy.54), calls=%async_computation | async-start | bytes 131072 | tf_op jit(solution)/shard_map/all_to_all | solution.py:159
  42.1 26.4 %copy-start.14 = (s32[2,12,2]{1,2,0:T(2,128)S(1)}, s32[2,12,2]{1,2,0:T(2,128)}, u32[]{:S(2)}) copy-start(s32[2,12,2]{1,2,0:T(2,128)} %param.15) | copy-start | bytes 580
  52.5 7.5 %all-to-all-start.2 = ((bf16[4,2,16,128]{3,2,1,0:T(8,128)(2,1)}), bf16[4,2,16,128]{3,2,1,0:T(8,128)(2,1)S(1)}, u32[]{:S(2)}, u32[]{:S(2)}) async-start(bf16[4,2,16,128]{3,2,1,0:T(8,128)(2,1)} %copy_bitcast_fusion), calls=%async_computation.2 | async-start | bytes 65536 | tf_op jit(solution)/shard_map/all_to_all | solution.py:37
  55.7 14.1 %copy-start.15 = (s32[2]{0:T(128)}, s32[2]{0:T(128)S(1)}, u32[]{:S(2)}) copy-start(s32[2]{0:T(128)S(1)} %iota_add_fusion) | copy-start | bytes 28
  58.1 11.9 %copy-start.12 = (s32[128]{0:T(128)}, s32[128]{0:T(128)S(1)}, u32[]{:S(2)}) copy-start(s32[128]{0:T(128)S(1)} %reduce.1) | copy-start | bytes 1540
  61.6 27.6 %all-to-all-start.3 = ((bf16[128,16,128]{2,1,0:T(8,128)(2,1)}), bf16[128,16,128]{2,1,0:T(8,128)(2,1)S(1)}, u32[]{:S(2)}, u32[]{:S(2)}) async-start(bf16[128,16,128]{2,1,0:T(8,128)(2,1)} %copy.62), calls=%async_computation.3 | async-start | bytes 1048576 | tf_op jit(solution)/shard_map/all_to_all | solution.py:179
  90.7 7.4 %copy-start.3 = (f32[6,64,128]{2,1,0:T(8,128)S(1)}, f32[6,64,128]{2,1,0:T(8,128)}, u32[]{:S(2)}) copy-start(f32[6,64,128]{2,1,0:T(8,128)} %param.12) | copy-start | bytes 589828
  90.7 31.5 %all-to-all-start.4 = ((bf16[4,128,16,128]{3,2,1,0:T(8,128)(2,1)}), bf16[4,128,16,128]{3,2,1,0:T(8,128)(2,1)}, u32[]{:S(2)}, u32[]{:S(2)}) async-start(bf16[4,128,16,128]{3,2,1,0:T(8,128)(2,1)} %broadcast_in_dim.76), calls=%async_computation.4 | async-start | bytes 4194304 | tf_op jit(solution)/shard_map/all_to_all | solution.py:20
  132.5 23.1 %copy-start.11 = (s32[24]{0:T(128)S(1)}, s32[24]{0:T(128)}, u32[]{:S(2)}) copy-start(s32[24]{0:T(128)} %copy-done.10) | copy-start | bytes 292
  132.5 23.1 %copy-start.20 = (s32[16]{0:T(128)S(1)}, s32[16]{0:T(128)}, u32[]{:S(2)}) copy-start(s32[16]{0:T(128)} %and_select_fusion) | copy-start | bytes 196
  135.4 1.7 copy-start.2
  145.0 1.7 copy-start.2
  151.7 10.4 %copy-start.22 = (bf16[2,128,512]{2,1,0:T(8,128)(2,1)}, bf16[2,128,512]{2,1,0:T(8,128)(2,1)S(1)}, u32[]{:S(2)}) copy-start(bf16[2,128,512]{2,1,0:T(8,128)(2,1)S(1)} %get-tuple-element.218) | copy-start | bytes 786436
  151.7 9.3 %copy-start.19 = (s32[24]{0:T(128)S(1)}, s32[24]{0:T(128)}, u32[]{:S(2)}) copy-start(s32[24]{0:T(128)} %copy-done.18) | copy-start | bytes 292
  152.4 7.5 %all-to-all-start.5 = ((bf16[4,2,16,128]{3,2,1,0:T(8,128)(2,1)}), bf16[4,2,16,128]{3,2,1,0:T(8,128)(2,1)S(1)}, u32[]{:S(2)}, u32[]{:S(2)}) async-start(bf16[4,2,16,128]{3,2,1,0:T(8,128)(2,1)} %copy.67), calls=%async_computation.5 | async-start | bytes 65536 | tf_op jit(solution)/shard_map/all_to_all | solution.py:37
  161.0 28.1 %copy-start.13 = (s32[128]{0:T(128)S(1)}, s32[128]{0:T(128)}, u32[]{:S(2)}) copy-start(s32[128]{0:T(128)} %copy-done.12) | copy-start | bytes 1540
  161.0 28.0 %copy-start.16 = (s32[2]{0:T(128)S(1)}, s32[2]{0:T(128)}, u32[]{:S(2)}) copy-start(s32[2]{0:T(128)} %copy-done.15) | copy-start | bytes 28
  161.7 34.7 %copy-start.7 = (bf16[64,512]{1,0:T(8,128)(2,1)S(1)}, bf16[64,512]{1,0:T(8,128)(2,1)}, u32[]{:S(2)}) copy-start(bf16[64,512]{1,0:T(8,128)(2,1)} %copy-done.6) | copy-start | bytes 196612
  162.1 34.8 %copy-start.4 = (bf16[512,512]{1,0:T(8,128)(2,1)S(1)}, bf16[512,512]{1,0:T(8,128)(2,1)}, u32[]{:S(2)}) copy-start(bf16[512,512]{1,0:T(8,128)(2,1)} %param.11) | copy-start | bytes 1572868
  (7 other events, 8.1 us)
where the time goes:
time: 217 us; the launch traced here: 216 us
  waiting for transfers between devices  65.5 us (30%)
  blocking collectives  51.2 us (24%)
  starting transfers between devices  46.3 us (21%)
  other arithmetic  25.3 us (12%)
  local copies, waits for them, and re-layouts  16 us (7%)
  matrix products  10.6 us (5%)
    all_to_all x2, waiting for transfers between devices, copy_for_each(): lax.all_to_all(jnp.broadcast_to(array[None], (devices, *array.shape)), ax...  30.8 us
    all_to_all x1, blocking collectives, local(): lax.all_to_all(returned.astype(jnp.bfloat16), 'ctx', split_axis=0, concat...  26.9 us
    all_to_all x1, starting transfers between devices, local(): lax.all_to_all(wanted[:, None], 'ctx', split_axis=0, concat_axis=0, tiled...  23.2 us
    all_to_all x1, waiting for transfers between devices, local(): lax.all_to_all(outgoing, 'ctx', split_axis=0, concat_axis=0, tiled=True)  19.2 us
    all_to_all x1, blocking collectives, summed_on_arrival(): lax.all_to_all(split_up(array, dim, devices), axis, 0, 0, tiled=True)  17.2 us
    all_to_all x2, starting transfers between devices, copy_for_each(): lax.all_to_all(jnp.broadcast_to(array[None], (devices, *array.shape)), ax...  9.61 us
    all_to_all x1, waiting for transfers between devices, local(): lax.all_to_all(wanted[:, None], 'ctx', split_axis=0, concat_axis=0, tiled...  9.49 us
    another operation x6, other arithmetic  7.39 us
  transfers between devices with their start and end apart: 6, of which 6 were waited for; matrix products, arithmetic and copies ran while one was open for 5% of the time, Pallas kernels for 0%

commit v1 on v0

v1 whole, which is shorter than its diff:
```python
import functools
import math

import jax
import jax.numpy as jnp
import ml_dtypes
import numpy as np
from jax import lax
from jax.experimental import pallas as pl
from jax.experimental.pallas import tpu as pltpu
from jax.sharding import PartitionSpec as P

STEEPNESS = 4.0
THRESHOLD = 1.0
N = 512
M = 64
K = 6
T = 4
R = N // T
Q = M // T
SIDE = 8
CTX = 2 * SIDE * SIDE
SRC = 12
PAIRS = 2 * SRC
MESH = pl.DeviceIdType.MESH
F32 = jnp.float32
BF16 = jnp.bfloat16
NEAR_FIRST = (1, 7, 2, 6, 3, 5, 4)


def tables():
    freq = (np.arange(M) - M // 2) % N
    angle = (freq[:, None] * np.arange(N)[None, :] % N) * (2.0 * math.pi / N)
    cos = np.cos(angle) / math.sqrt(N)
    sin = np.sin(angle) / math.sqrt(N)
    fst = np.concatenate([cos, -sin], 0)
    gcat = np.concatenate([cos.T, sin.T], 1)
    inv = np.concatenate([np.concatenate([cos, sin], 1), np.concatenate([-sin, cos], 1)], 0)
    adj = np.concatenate([np.concatenate([cos.T, -sin.T], 1), np.concatenate([sin.T, cos.T], 1)], 0)
    adj = np.concatenate([adj, -adj[:, M:], adj[:, :M]], 1)
    order = np.arange(2 * N).reshape(2, T, N // T).transpose(1, 0, 2).reshape(-1)
    return [t.astype(ml_dtypes.bfloat16) for t in (fst, gcat, inv[:, order], adj[order])]


def sine_coefficients():
    w = 0.25 * np.cos(np.pi * (np.arange(400) + 0.5) / 400)
    powers = np.stack([w ** (2 * i + 1) for i in range(6)], 1)
    return [float(c) for c in np.linalg.lstsq(powers, np.sin(2 * np.pi * w), rcond=None)[0]]


SINE = sine_coefficients()


def swap(a):
    return pltpu.roll(a, M, 1)


def left_half(shape):
    return lax.broadcasted_iota(jnp.int32, shape, 1) < M


def turn_rates(tile):
    row = lax.broadcasted_iota(jnp.int32, (Q, 2 * M), 0) + (tile * Q - M // 2)
    lane = lax.broadcasted_iota(jnp.int32, (Q, 2 * M), 1)
    col = lane % M - M // 2
    late = jnp.where(lane < M, 0.0, 0.25).astype(F32)
    return row.astype(F32) * (1.0 / N), col.astype(F32) * (1.0 / N), late


def cos_sin(rates, r, s):
    y = rates[0] * r + rates[1] * s - rates[2]
    y = y - jnp.floor(y + 0.5)
    w = 0.25 - jnp.abs(y)
    z = w * w
    total = jnp.full_like(z, SINE[-1])
    for c in SINE[-2::-1]:
        total = total * z + c
    return total * w


def dot(a, b, dims=((1,), (0,))):
    return lax.dot_general(a, b, (dims, ((), ())), preferred_element_type=F32)


def wait_all(copies):
    for c in copies:
        c.wait()


def main_kernel(
    masks, br, bc, pupils, targets, ids_s, ids_v, fst, gcat, inv, adj,
    resist, g2, ids_all, p_out, q_out,
    g1, part, part_in, spec, prr, pii, amp, u_all, pull, phases,
    x_send, x_recv, a_send, a_recv, i_send, i_recv,
):
    tile = lax.axis_index("tile")
    q = lax.axis_index("ctx")
    core, y, z = q % 2, (q // 2) % SIDE, q // (2 * SIDE)
    major = z + core * (y - z)
    minor = y + core * (z - y)

    def ctx_id(mj, mn):
        zz = mj + core * (mn - mj)
        yy = mn + core * (mj - mn)
        return zz * (2 * SIDE) + yy * 2 + core

    sibling = q + 1 - 2 * core
    barrier = pltpu.get_barrier_semaphore()
    for k in range(1, T):
        pl.semaphore_signal(barrier, inc=1, device_id={"tile": (tile + k) % T}, device_id_type=MESH)
    for k in range(1, SIDE):
        pl.semaphore_signal(barrier, inc=1, device_id={"ctx": ctx_id(major, (minor + k) % SIDE)}, device_id_type=MESH)
        pl.semaphore_signal(barrier, inc=1, device_id={"ctx": ctx_id((major + k) % SIDE, minor)}, device_id_type=MESH)
    pl.semaphore_signal(barrier, inc=1, device_id={"ctx": sibling}, device_id_type=MESH)

    own = pl.ds(pl.multiple_of(tile * R, R), R)
    table = fst[...]
    p_st = dot(table, br[:, own]).astype(BF16)
    q_f = dot(table, bc[...])
    q_st = q_f.astype(BF16)
    p_out[...] = p_st
    q_out[...] = q_st
    qq = jnp.concatenate([q_st, -q_st[M:], q_st[:M]], 0)
    pcat = jnp.concatenate([p_st[:M], p_st[M:]], 1)
    for m in range(2):
        a = dot(masks[m], qq, ((1,), (1,))).astype(BF16)
        s = dot(pcat, jnp.concatenate([a[:, : 2 * M], a[:, 2 * M :]], 0))
        for t in range(T):
            part[0, t, m * Q : (m + 1) * Q] = s[t * Q : (t + 1) * Q]

    pl.semaphore_wait(barrier, T - 1 + 2 * (SIDE - 1) + 1)

    def tile_scatter(step):
        copies = []
        for k in range(1, T):
            to = (tile + k) % T
            copies.append(
                pltpu.make_async_remote_copy(
                    src_ref=part.at[step, to], dst_ref=part_in.at[step, k - 1],
                    send_sem=x_send.at[2 * step, k - 1], recv_sem=x_recv.at[2 * step, k - 1],
                    device_id={"tile": to}, device_id_type=MESH,
                )
            )
        for c in copies:
            c.start()
        return copies

    def tile_sum(step):
        return (part[step, tile] + part_in[step, 0]) + (part_in[step, 1] + part_in[step, 2])

    def line_copies(buf, unit, send, recv, phase):
        half = core * (SIDE * SIDE)
        copies = []
        for k in NEAR_FIRST:
            if phase == 0:
                place = pl.ds((half + major * SIDE + minor) * unit, unit)
                to = ctx_id(major, (minor + k) % SIDE)
            else:
                place = pl.ds((half + major * SIDE) * unit, SIDE * unit)
                to = ctx_id((major + k) % SIDE, minor)
            copies.append(
                pltpu.make_async_remote_copy(
                    src_ref=buf.at[place], dst_ref=buf.at[place],
                    send_sem=send.at[phase, k], recv_sem=recv.at[phase, k],
                    device_id={"ctx": to}, device_id_type=MESH,
                )
            )
        for c in copies:
            c.start()
        return copies

    def sibling_copy(buf, unit, send, recv, k):
        row = (major + SIDE - k) % SIDE
        place = pl.ds((core * (SIDE * SIDE) + row * SIDE) * unit, SIDE * unit)
        copy = pltpu.make_async_remote_copy(
            src_ref=buf.at[place], dst_ref=buf.at[place],
            send_sem=send.at[2, k], recv_sem=recv.at[2, k],
            device_id={"ctx": sibling}, device_id_type=MESH,
        )
        copy.start()
        return copy

    def gather(bufs, between):
        first = [line_copies(b, u, s, r, 0) for b, u, s, r in bufs]
        between()
        for f in first:
            wait_all(f)
        second = [line_copies(b, u, s, r, 1) for b, u, s, r in bufs]
        third = [sibling_copy(b, u, s, r, 0) for b, u, s, r in bufs]
        for i, k in enumerate(NEAR_FIRST):
            for (b, u, s, r), copies in zip(bufs, second):
                copies[i].wait()
                third.append(sibling_copy(b, u, s, r, k))
        wait_all(third)

    copies = tile_scatter(0)

    rates = turn_rates(tile)
    for p in range(PAIRS):
        r = ids_s[0, PAIRS + 2 * p].astype(F32)
        s = ids_s[0, PAIRS + 2 * p + 1].astype(F32)
        phases[p] = cos_sin(rates, r, s)
    left64 = left_half((M, 2 * M))
    for k in range(K):
        pk = pupils[k]
        turned = swap(pk)
        prr[k] = jnp.where(left64, pk, turned)
        pii[k] = jnp.where(left64, -turned, pk)

    slot = core * (SIDE * SIDE) + major * SIDE + minor
    wait_all(copies)
    g1[pl.ds(slot * 2, 2)] = tile_sum(0).astype(BF16).reshape(2, Q, 2 * M)
    ids_all[pl.ds(slot, 1)] = ids_v[...]
    gather([(g1, 2, a_send.at[0], a_recv.at[0]), (ids_all, 1, i_send, i_recv)], lambda: None)

    leftq = left_half((Q, 2 * M))
    for c in range(2):
        sum_a = jnp.zeros((Q, 2 * M), F32)
        sum_b = jnp.zeros((Q, 2 * M), F32)
        for j in range(SRC):
            p = c * SRC + j
            master = ids_s[0, p]
            owner = master >> 1
            ocore = owner & 1
            oy = (owner >> 1) & (SIDE - 1)
            oz = owner >> 4
            place = ocore * (SIDE * SIDE) + oz * SIDE + oy + ocore * (SIDE - 1) * (oy - oz)
            g = g1[place * 2 + (master & 1)].astype(F32)
            cs = phases[p]
            sum_a += g * cs
            sum_b += swap(g) * cs
        spec[tile, c * Q : (c + 1) * Q] = jnp.where(leftq, sum_a + swap(sum_a), swap(sum_b) - sum_b)
    copies = []
    for k in range(1, T):
        copies.append(
            pltpu.make_async_remote_copy(
                src_ref=spec.at[tile], dst_ref=spec.at[tile],
                send_sem=x_send.at[1, k - 1], recv_sem=x_recv.at[1, k - 1],
                device_id={"tile": (tile + k) % T}, device_id_type=MESH,
            )
        )
    for c in copies:
        c.start()
    wait_all(copies)

    fown = fst[:, own]
    fcat = jnp.concatenate([fown[:M], fown[M:]], 1)
    gown = gcat[own, :]
    for c in range(2):
        s = jnp.concatenate([spec[t, c * Q : (c + 1) * Q] for t in range(T)], 0)
        s_sw = swap(s)
        s2 = jnp.where(left64, -s_sw, s_sw)
        s2_sw = jnp.where(left64, s, -s)
        for k in range(K):
            a1 = prr[k] * s + pii[k] * s_sw
            a2 = prr[k] * s2 + pii[k] * s2_sw
            both = jnp.concatenate([a1, a2], 0).astype(BF16)
            u_all[k * R : (k + 1) * R] = dot(gown, both).astype(BF16)
        for b in range(T):
            cols = slice(b * R, (b + 1) * R)
            field = dot(u_all[...], inv[:, b * 2 * R : (b + 1) * 2 * R])
            intensity = jnp.zeros((R, R), F32)
            for k in range(K):
                fr = field[k * R : (k + 1) * R, :R]
                fi = field[k * R : (k + 1) * R, R:]
                intensity += fr * fr + fi * fi
            image = 1.0 / (1.0 + jnp.exp(-STEEPNESS * (intensity - THRESHOLD)))
            resist[c, :, cols] = image.astype(BF16)
            slope = (image - targets[c, :, cols].astype(F32)) * (2.0 * STEEPNESS) * image * (1.0 - image)
            slope2 = jnp.concatenate([slope, slope], 1)
            for k in range(K):
                pull[k * R : (k + 1) * R, b * 2 * R : (b + 1) * 2 * R] = (
                    slope2 * field[k * R : (k + 1) * R]
                ).astype(BF16)
        folded = dot(pull[...], adj[...]).astype(BF16)
        g_a = jnp.zeros((M, 2 * M), F32)
        g_b = jnp.zeros((M, 2 * M), F32)
        for k in range(K):
            fk = folded[k * R : (k + 1) * R]
            ga = dot(fcat, jnp.concatenate([fk[:, : 2 * M], fk[:, 2 * M :]], 0))
            g_a += prr[k] * ga
            g_b += pii[k] * ga
        grad = g_a + swap(g_b)
        for t in range(T):
            part[1, t, c * Q : (c + 1) * Q] = grad[t * Q : (t + 1) * Q]

    wait_all(tile_scatter(1))
    g2[pl.ds(slot * 2, 2)] = tile_sum(1).astype(BF16).reshape(2, Q, 2 * M)
    gather([(g2, 2, a_send.at[1], a_recv.at[1])], lambda: None)


def pair_kernel(where_s, ids_s, ids_v, g2, out, lists_v, lists_s, acc, sem):
    me = where_s[0]
    rates = turn_rates(where_s[1])
    ids = ids_v[...].reshape(CTX, 128)
    lane = lax.broadcasted_iota(jnp.int32, (CTX, 128), 1)
    sub = lax.broadcasted_iota(jnp.int32, (CTX, 128), 0)
    sub8 = lax.broadcasted_iota(jnp.int32, (8, 128), 0)
    lane8 = lax.broadcasted_iota(jnp.int32, (8, 128), 1)
    weights = jnp.where(sub8 == 0, 1, jnp.where(sub8 == 1, lane8, 0)).astype(F32).astype(BF16)
    before = jnp.where(sub < lane, 1.0, 0.0).astype(BF16)
    for m in range(2):
        match = jnp.where((ids == 2 * me + m) & (lane < PAIRS), 1.0, 0.0).astype(BF16)
        stats = dot(weights, match, ((1,), (1,)))
        count = jnp.broadcast_to(stats[0:1], (8, 128))
        index = jnp.broadcast_to(stats[1:2], (8, 128))
        single = jnp.where(count == 1.0, 1.0, 0.0)
        rank = dot(single.astype(BF16), before)
        hot = jnp.where(
            (jnp.broadcast_to(rank[0:1], (CTX, 128)) == sub.astype(F32))
            & (jnp.broadcast_to(single[0:1], (CTX, 128)) > 0.5),
            1.0, 0.0,
        ).astype(BF16)
        load = jnp.where(sub8 == 0, lane8.astype(F32), jnp.where(sub8 == 1, index * single, jnp.where(sub8 == 2, 1.0, 0.0)))
        listed = dot(load.astype(BF16), hot, ((1,), (1,)))
        n_single = jnp.sum(single, axis=1, keepdims=True)
        n_multi = jnp.sum(jnp.where(count > 1.5, 1.0, 0.0), axis=1, keepdims=True)
        rows = jnp.where(sub8 == 3, n_single, jnp.where(sub8 == 4, n_multi, jnp.where(sub8 == 5, count, listed)))
        lists_v[m * 8 : (m + 1) * 8] = rows.astype(jnp.int32)
    copy = pltpu.make_async_copy(lists_v, lists_s, sem)
    copy.start()
    copy.wait()

    def terms(h, j, weight):
        r = ids_s[h, 0, PAIRS + 2 * j].astype(F32)
        s = ids_s[h, 0, PAIRS + 2 * j + 1].astype(F32)
        g = g2[2 * h + j // SRC].astype(F32)
        cs = cos_sin(rates, r, s)
        if weight is not None:
            cs = cs * weight
        return g * cs, swap(g) * cs

    block = 8
    left = left_half((Q, 2 * M))
    for m in range(2):

        def step(i, carry):
            sum_a, sum_b = carry
            for b in range(block):
                k = i * block + b
                add_a, add_b = terms(
                    lists_s[m * 8, k], lists_s[m * 8 + 1, k], lists_s[m * 8 + 2, k].astype(F32)
                )
                sum_a += add_a
                sum_b += add_b
            return sum_a, sum_b

        zero = jnp.zeros((Q, 2 * M), F32)
        sum_a, sum_b = lax.fori_loop(0, (lists_s[m * 8 + 3, 0] + block - 1) // block, step, (zero, zero))
        acc[0] = sum_a
        acc[1] = sum_b

        @pl.when(lists_s[m * 8 + 4, 0] > 0)
        def _():
            def host(h, _):
                @pl.when(lists_s[m * 8 + 5, h] > 1)
                def _():
                    def one(j, _):
                        @pl.when(ids_s[h, 0, j] == 2 * me + m)
                        def _():
                            add_a, add_b = terms(h, j, None)
                            acc[0] += add_a
                            acc[1] += add_b

                        return 0

                    lax.fori_loop(0, PAIRS, one, 0)

                return 0

            lax.fori_loop(0, CTX, host, 0)

        sum_a, sum_b = acc[0], acc[1]
        out[m * Q : (m + 1) * Q] = jnp.where(left, sum_a - swap(sum_a), sum_b + swap(sum_b)).astype(BF16)


def last_kernel(gq, p_st, q_st, out, rows, x_send, x_recv):
    tile = lax.axis_index("tile")
    barrier = pltpu.get_barrier_semaphore()
    for k in range(1, T):
        pl.semaphore_signal(barrier, inc=1, device_id={"tile": (tile + k) % T}, device_id_type=MESH)
    rows[tile] = gq[...]
    pl.semaphore_wait(barrier, T - 1)
    copies = []
    for k in range(1, T):
        copies.append(
            pltpu.make_async_remote_copy(
                src_ref=rows.at[tile], dst_ref=rows.at[tile],
                send_sem=x_send.at[k - 1], recv_sem=x_recv.at[k - 1],
                device_id={"tile": (tile + k) % T}, device_id_type=MESH,
            )
        )
    for c in copies:
        c.start()
    wait_all(copies)
    left = left_half((M, 2 * M))
    for m in range(2):
        g = jnp.concatenate([rows[t, m * Q : (m + 1) * Q].astype(F32) for t in range(T)], 0)
        turned = swap(g)
        both = jnp.concatenate([g, jnp.where(left, turned, -turned)], 0).astype(BF16)
        lifted = dot(p_st[...], both, ((0,), (0,))).astype(BF16)
        out[m] = dot(lifted, q_st[...])


def local(masks, blur_rows, blur_cols, pupils, targets, context_masters, offsets):
    vmem = pl.BlockSpec(memory_space=pltpu.VMEM)
    smem = pl.BlockSpec(memory_space=pltpu.SMEM)
    dma = pltpu.SemaphoreType.DMA
    packed = jnp.concatenate(
        [context_masters.reshape(-1), offsets.reshape(-1), jnp.zeros((128 - 3 * PAIRS,), jnp.int32)]
    ).reshape(1, 128)
    resist, g2, ids_all, p_st, q_st = pl.pallas_call(
        main_kernel,
        out_shape=(
            jax.ShapeDtypeStruct((2, R, N), BF16),
            jax.ShapeDtypeStruct((2 * CTX, Q, 2 * M), BF16),
            jax.ShapeDtypeStruct((CTX, 1, 128), jnp.int32),
            jax.ShapeDtypeStruct((2 * M, R), BF16),
            jax.ShapeDtypeStruct((2 * M, N), BF16),
        ),
        in_specs=[vmem] * 5 + [smem] + [vmem] * 5,
        out_specs=(vmem,) * 5,
        scratch_shapes=[
            pltpu.VMEM((2 * CTX, Q, 2 * M), BF16),
            pltpu.VMEM((2, T, 2 * Q, 2 * M), F32),
            pltpu.VMEM((2, T - 1, 2 * Q, 2 * M), F32),
            pltpu.VMEM((T, 2 * Q, 2 * M), F32),
            pltpu.VMEM((K, M, 2 * M), F32),
            pltpu.VMEM((K, M, 2 * M), F32),
            pltpu.VMEM((8, 128), F32),
            pltpu.VMEM((K * R, 2 * M), BF16),
            pltpu.VMEM((K * R, 2 * N), BF16),
            pltpu.VMEM((PAIRS, Q, 2 * M), F32),
            dma((3, T - 1)),
            dma((3, T - 1)),
            dma((2, 3, SIDE)),
            dma((2, 3, SIDE)),
            dma((3, SIDE)),
            dma((3, SIDE)),
        ],
        compiler_params=pltpu.CompilerParams(
            collective_id=0, has_side_effects=True, vmem_limit_bytes=48 << 20
        ),
        name="main",
    )(masks, blur_rows, blur_cols, pupils, targets, packed, packed.reshape(1, 1, 128), *tables())
    where = jnp.stack([lax.axis_index("ctx"), lax.axis_index("tile")]).astype(jnp.int32)
    gq = pl.pallas_call(
        pair_kernel,
        out_shape=jax.ShapeDtypeStruct((2 * Q, 2 * M), BF16),
        in_specs=[smem, smem, vmem, vmem],
        out_specs=vmem,
        scratch_shapes=[
            pltpu.VMEM((16, 128), jnp.int32),
            pltpu.SMEM((16, 128), jnp.int32),
            pltpu.VMEM((2, Q, 2 * M), F32),
            dma,
        ],
        compiler_params=pltpu.CompilerParams(vmem_limit_bytes=32 << 20),
        name="pairs",
    )(where, ids_all, ids_all, g2)
    mask_grad = pl.pallas_call(
        last_kernel,
        out_shape=jax.ShapeDtypeStruct((2, R, N), F32),
        in_specs=[vmem] * 3,
        out_specs=vmem,
        scratch_shapes=[pltpu.VMEM((T, 2 * Q, 2 * M), BF16), dma((T - 1,)), dma((T - 1,))],
        compiler_params=pltpu.CompilerParams(
            collective_id=1, has_side_effects=True, vmem_limit_bytes=32 << 20
        ),
        name="last",
    )(gq, p_st, q_st)
    return (resist, mask_grad)


def solution(mesh):
    placed = (
        P("ctx", "tile", None),
        P(),
        P(),
        P(),
        P("ctx", "tile", None),
        P("ctx", None),
        P("ctx", None, None),
    )
    return jax.shard_map(
        local,
        mesh=mesh,
        in_specs=placed,
        out_specs=(P("ctx", "tile", None), P("ctx", "tile", None)),
        check_vma=False,
    )
```

time: 217 us -> 86.1 us (0.40)
  the two profiles are of different devices: /device:TPU:1 before, /device:TPU:16 now
where the time goes in v1:
time: 86.1 us; the launch traced here: 85.6 us
  Pallas kernels  72.9 us (85%)
  local copies, waits for them, and re-layouts  11.7 us (14%)
    pallas_call x1, Pallas kernels, local(): pl.pallas_call(main_kernel, out_shape=(jax.ShapeDtypeStruct((2, R, N), BF...  61.2 us
    unnamed x23, local copies, waits for them, and re-layouts  11.6 us
    pallas_call x1, Pallas kernels, local(): pl.pallas_call(last_kernel, out_shape=jax.ShapeDtypeStruct((2, R, N), F32...  6.54 us
    pallas_call x1, Pallas kernels, local(): pl.pallas_call(pair_kernel, out_shape=jax.ShapeDtypeStruct((2 * Q, 2 * M)...  5.2 us

profile of v1, /device:TPU:16, one launch (start us, length us, event | category | flops | bytes accessed | tf_op | source)
XLA Modules:
  0.0 85.6 jit_solution(14600994152575815749)
XLA Ops:
  0.6 0.8 copy.14
  1.4 0.0 copy-start.9
  1.4 0.1 reshape.14
  1.5 0.6 copy-done.9
  2.1 0.1 reshape.13
  2.2 0.1 fusion.ids_v
  2.2 0.1 fusion.1.ids_s
  2.3 0.0 copy-start
  2.3 1.0 %copy-done = bf16[512,512]{1,0:T(8,128)(2,1)S(1)} copy-done((bf16[512,512]{1,0:T(8,128)(2,1)S(1)}, bf16[512,512]{1,0:T(8,128)(2,1)}, u32[]{:S(2)}) %copy-start) | copy-done | bytes 524312
  3.4 0.0 copy-start.1
  3.4 1.0 %copy-done.1 = bf16[512,512]{1,0:T(8,128)(2,1)S(1)} copy-done((bf16[512,512]{1,0:T(8,128)(2,1)S(1)}, bf16[512,512]{1,0:T(8,128)(2,1)}, u32[]{:S(2)}) %copy-start.1) | copy-done | bytes 524312
  4.4 1.0 %copy-done.2 = bf16[1024,256]{1,0:T(8,128)(2,1)S(1)} copy-done((bf16[1024,256]{1,0:T(8,128)(2,1)S(1)}, bf16[1024,256]{1,0:T(8,128)(2,1)}, u32[]{:S(2)}) %copy-start.2) | copy-done | bytes 524312
  5.5 0.9 %copy-done.3 = bf16[2,128,512]{2,1,0:T(8,128)(2,1)S(1)} copy-done((bf16[2,128,512]{2,1,0:T(8,128)(2,1)S(1)}, bf16[2,128,512]{2,1,0:T(8,128)(2,1)}, u32[]{:S(2)}) %copy-start.3) | copy-done | bytes 262168
  6.4 0.9 %copy-done.4 = bf16[2,128,512]{2,1,0:T(8,128)(2,1)S(1)} copy-done((bf16[2,128,512]{2,1,0:T(8,128)(2,1)S(1)}, bf16[2,128,512]{2,1,0:T(8,128)(2,1)}, u32[]{:S(2)}) %copy-start.4) | copy-done | bytes 262168
  7.4 0.9 %copy-done.5 = bf16[128,1024]{1,0:T(8,128)(2,1)S(1)} copy-done((bf16[128,1024]{1,0:T(8,128)(2,1)S(1)}, bf16[128,1024]{1,0:T(8,128)(2,1)}, u32[]{:S(2)}) %copy-start.5) | copy-done | bytes 262168
  8.3 0.9 %copy-done.6 = f32[6,64,128]{2,1,0:T(8,128)S(1)} copy-done((f32[6,64,128]{2,1,0:T(8,128)S(1)}, f32[6,64,128]{2,1,0:T(8,128)}, u32[]{:S(2)}) %copy-start.6) | copy-done | bytes 196632
  9.2 0.9 %copy-done.7 = bf16[128,512]{1,0:T(8,128)(2,1)S(1)} copy-done((bf16[128,512]{1,0:T(8,128)(2,1)S(1)}, bf16[128,512]{1,0:T(8,128)(2,1)}, u32[]{:S(2)}) %copy-start.7) | copy-done | bytes 131096
  10.1 0.9 %copy-done.8 = bf16[512,128]{1,0:T(8,128)(2,1)S(1)} copy-done((bf16[512,128]{1,0:T(8,128)(2,1)S(1)}, bf16[512,128]{1,0:T(8,128)(2,1)}, u32[]{:S(2)}) %copy-start.8) | copy-done | bytes 131096
  11.0 61.2 %main.1 = (bf16[2,128,512]{2,1,0:T(8,128)(2,1)S(1)}, bf16[256,16,128]{2,1,0:T(8,128)(2,1)S(1)}, s32[128,1,128]{2,1,0:T(1,128)S(1)}, bf16[128,128]{1,0:T(8,128)(2,1)S(1)}, bf16[128,512]{1,0:T(8,128)(2,1)S(1)}) custom-call(bf16[2,128,512]{2,1,0:T(8,128)(2,1)S(1)} %copy-done.3, bf16[512,512]{1,0:T(8,128)(2,1)S(1)} %copy-done, bf16[512,512]{1,0:T(8,128)(2,1)S(1)} %copy-done.1, ...), custom_call_target="tpu_custom_call" | custom-call | tf_op jit(solution)/shard_map/main/pallas_call | solution.py:412
  72.3 0.1 pad_add_fusion.1.where_s
  72.3 5.2 %pairs.1.gq = bf16[32,128]{1,0:T(8,128)(2,1)S(1)} custom-call(s32[2]{0:T(128)S(1)} %pad_add_fusion.1.where_s, s32[128,1,128]{2,1,0:T(1,128)S(1)} %get-tuple-element.8.ids_s.ids_v, s32[128,1,128]{2,1,0:T(1,128)S(1)} %get-tuple-element.8.ids_s.ids_v, bf16[256,16,128]{2,1,0:T(8,128)(2,1)S(1)} %get-tuple-element.9.g2), custom_call_target="tpu_custom_call" | custom-call | tf_op jit(solution)/shard_map/pairs/pallas_call | solution.py:447
  77.5 6.5 %last.1 = f32[2,128,512]{2,1,0:T(8,128)S(1)} custom-call(bf16[32,128]{1,0:T(8,128)(2,1)S(1)} %pairs.1.gq, bf16[128,128]{1,0:T(8,128)(2,1)S(1)} %get-tuple-element.10.p_st, bf16[128,512]{1,0:T(8,128)(2,1)S(1)} %get-tuple-element.11.q_st), custom_call_target="tpu_custom_call" | custom-call | tf_op jit(solution)/shard_map/last/pallas_call | solution.py:461
  84.1 0.7 copy.17
  84.8 0.8 copy.18
  (8 shorter events, 0.0 us)
Async XLA Ops:
  1.4 0.7 copy-start.9
  2.3 1.0 %copy-start = (bf16[512,512]{1,0:T(8,128)(2,1)S(1)}, bf16[512,512]{1,0:T(8,128)(2,1)}, u32[]{:S(2)}) copy-start(bf16[512,512]{1,0:T(8,128)(2,1)} %br.1) | copy-start | bytes 1572868
  3.4 1.0 %copy-start.1 = (bf16[512,512]{1,0:T(8,128)(2,1)S(1)}, bf16[512,512]{1,0:T(8,128)(2,1)}, u32[]{:S(2)}) copy-start(bf16[512,512]{1,0:T(8,128)(2,1)} %bc.1) | copy-start | bytes 1572868
  4.4 1.0 %copy-start.2 = (bf16[1024,256]{1,0:T(8,128)(2,1)S(1)}, bf16[1024,256]{1,0:T(8,128)(2,1)}, u32[]{:S(2)}) copy-start(bf16[1024,256]{1,0:T(8,128)(2,1)} %constant.22.clone.adj) | copy-start | bytes 1572868
  5.5 0.9 %copy-start.3 = (bf16[2,128,512]{2,1,0:T(8,128)(2,1)S(1)}, bf16[2,128,512]{2,1,0:T(8,128)(2,1)}, u32[]{:S(2)}) copy-start(bf16[2,128,512]{2,1,0:T(8,128)(2,1)} %masks.1) | copy-start | bytes 786436
  6.4 0.9 %copy-start.4 = (bf16[2,128,512]{2,1,0:T(8,128)(2,1)S(1)}, bf16[2,128,512]{2,1,0:T(8,128)(2,1)}, u32[]{:S(2)}) copy-start(bf16[2,128,512]{2,1,0:T(8,128)(2,1)} %targets.1) | copy-start | bytes 786436
  7.4 0.9 %copy-start.5 = (bf16[128,1024]{1,0:T(8,128)(2,1)S(1)}, bf16[128,1024]{1,0:T(8,128)(2,1)}, u32[]{:S(2)}) copy-start(bf16[128,1024]{1,0:T(8,128)(2,1)} %constant.21.clone.inv) | copy-start | bytes 786436
  8.3 0.9 %copy-start.6 = (f32[6,64,128]{2,1,0:T(8,128)S(1)}, f32[6,64,128]{2,1,0:T(8,128)}, u32[]{:S(2)}) copy-start(f32[6,64,128]{2,1,0:T(8,128)} %pupils.1) | copy-start | bytes 589828
  9.2 0.9 %copy-start.7 = (bf16[128,512]{1,0:T(8,128)(2,1)S(1)}, bf16[128,512]{1,0:T(8,128)(2,1)}, u32[]{:S(2)}) copy-start(bf16[128,512]{1,0:T(8,128)(2,1)} %constant.19.clone.fst) | copy-start | bytes 393220
  10.1 0.9 %copy-start.8 = (bf16[512,128]{1,0:T(8,128)(2,1)S(1)}, bf16[512,128]{1,0:T(8,128)(2,1)}, u32[]{:S(2)}) copy-start(bf16[512,128]{1,0:T(8,128)(2,1)} %constant.20.clone.gcat) | copy-start | bytes 393220

commit v2 on v1

--- a/solution.py
+++ b/solution.py
@@ -87,17 +87,85 @@
         c.wait()
 
 
+def near_first(i):
+    return (i % 2) * ((i + 1) // 2) + (1 - i % 2) * (SIDE - i // 2)
+
+
+def pair_lists(ids, me):
+    lane = lax.broadcasted_iota(jnp.int32, (CTX, 128), 1)
+    sub = lax.broadcasted_iota(jnp.int32, (CTX, 128), 0)
+    sub8 = lax.broadcasted_iota(jnp.int32, (8, 128), 0)
+    lane8 = lax.broadcasted_iota(jnp.int32, (8, 128), 1).astype(F32)
+    ones = jnp.full((8, 128), 1.0, BF16)
+    before = jnp.where(sub < lane, 1.0, 0.0).astype(BF16)
+    r = pltpu.roll(ids, 128 - 32, 1)
+    s = pltpu.roll(ids, 128 - 64, 1)
+    second = jnp.where(lane >= SRC, 1.0, 0.0)
+    values = [second] + [v.astype(F32) for v in (r >> 4, r & 15, s >> 4, s & 15)]
+    lists = []
+    for m in range(2):
+        match = jnp.where((ids == 2 * me + m) & (lane < PAIRS), 1.0, 0.0)
+        count = dot(ones, match.astype(BF16), ((1,), (1,)))
+        found = [dot(ones, (match * v).astype(BF16), ((1,), (1,))) for v in values]
+        single = jnp.where(count == 1.0, 1.0, 0.0)
+        rank = dot(single.astype(BF16), before)
+        hot = jnp.where(
+            (jnp.broadcast_to(rank[0:1], (CTX, 128)) == sub.astype(F32))
+            & (jnp.broadcast_to(single[0:1], (CTX, 128)) > 0.5),
+            1.0, 0.0,
+        ).astype(BF16)
+        load = jnp.where(sub8 == 5, single, 0.0)
+        load = jnp.where(sub8 == 0, single * (2.0 * lane8 + found[0]), load)
+        for i in range(1, 5):
+            load = jnp.where(sub8 == i, single * found[i], load)
+        listed = dot(load.astype(BF16), hot, ((1,), (1,)))
+        line = [jnp.broadcast_to(listed[i : i + 1], (8, 128)) for i in range(6)]
+        n_single = jnp.sum(single, axis=1, keepdims=True)
+        n_multi = jnp.sum(jnp.where(count > 1.5, 1.0, 0.0), axis=1, keepdims=True)
+        rows = jnp.where(sub8 == 6, count, line[0])
+        rows = jnp.where(sub8 == 1, 16.0 * line[1] + line[2], rows)
+        rows = jnp.where(sub8 == 2, 16.0 * line[3] + line[4], rows)
+        rows = jnp.where(sub8 == 3, line[5], rows)
+        rows = jnp.where(sub8 == 4, n_single, rows)
+        rows = jnp.where(sub8 == 5, n_multi, rows)
+        lists.append(rows.astype(jnp.int32))
+    return lists
+
+
 def main_kernel(
-    masks, br, bc, pupils, targets, ids_s, ids_v, fst, gcat, inv, adj,
-    resist, g2, ids_all, p_out, q_out,
-    g1, part, part_in, spec, prr, pii, amp, u_all, pull, phases,
-    x_send, x_recv, a_send, a_recv, i_send, i_recv,
+    masks_h, br_h, bc_h, pupils_h, targets_h, ids_s, ids_v, fst_h, gcat_h, inv_h, adj_h,
+    resist, g2, ids_all, lists, p_out, q_out,
+    masks, br, bc, pupils, targets, fst, gown_v, inv, adj,
+    g1, part, part_in, spec, prr, pii, u_all, pull, phases,
+    load_sem, x_send, x_recv, a_send, a_recv, f_send, f_recv, s_send, s_recv, i_send, i_recv,
 ):
     tile = lax.axis_index("tile")
     q = lax.axis_index("ctx")
     core, y, z = q % 2, (q // 2) % SIDE, q // (2 * SIDE)
     major = z + core * (y - z)
     minor = y + core * (z - y)
+    half = core * (SIDE * SIDE)
+    slot = half + major * SIDE + minor
+    own = pl.ds(pl.multiple_of(tile * R, R), R)
+
+    loads = [
+        pltpu.make_async_copy(src, dst, load_sem.at[i])
+        for i, (src, dst) in enumerate(
+            [
+                (fst_h, fst),
+                (br_h.at[:, own], br),
+                (bc_h, bc),
+                (masks_h, masks),
+                (pupils_h, pupils),
+                (gcat_h.at[own, :], gown_v),
+                (inv_h, inv),
+                (targets_h, targets),
+                (adj_h, adj),
+            ]
+        )
+    ]
+    for copy in loads:
+        copy.start()
 
     def ctx_id(mj, mn):
         zz = mj + core * (mn - mj)
@@ -106,22 +174,24 @@
 
     sibling = q + 1 - 2 * core
     barrier = pltpu.get_barrier_semaphore()
-    for k in range(1, T):
-        pl.semaphore_signal(barrier, inc=1, device_id={"tile": (tile + k) % T}, device_id_type=MESH)
     for k in range(1, SIDE):
         pl.semaphore_signal(barrier, inc=1, device_id={"ctx": ctx_id(major, (minor + k) % SIDE)}, device_id_type=MESH)
         pl.semaphore_signal(barrier, inc=1, device_id={"ctx": ctx_id((major + k) % SIDE, minor)}, device_id_type=MESH)
+    for k in range(1, T):
+        pl.semaphore_signal(barrier, inc=1, device_id={"tile": (tile + k) % T}, device_id_type=MESH)
     pl.semaphore_signal(barrier, inc=1, device_id={"ctx": sibling}, device_id_type=MESH)
 
-    own = pl.ds(pl.multiple_of(tile * R, R), R)
+    loads[0].wait()
+    loads[1].wait()
     table = fst[...]
-    p_st = dot(table, br[:, own]).astype(BF16)
-    q_f = dot(table, bc[...])
-    q_st = q_f.astype(BF16)
+    p_st = dot(table, br[...]).astype(BF16)
+    loads[2].wait()
+    q_st = dot(table, bc[...]).astype(BF16)
     p_out[...] = p_st
     q_out[...] = q_st
     qq = jnp.concatenate([q_st, -q_st[M:], q_st[:M]], 0)
     pcat = jnp.concatenate([p_st[:M], p_st[M:]], 1)
+    loads[3].wait()
     for m in range(2):
         a = dot(masks[m], qq, ((1,), (1,))).astype(BF16)
         s = dot(pcat, jnp.concatenate([a[:, : 2 * M], a[:, 2 * M :]], 0))
@@ -148,70 +218,108 @@
     def tile_sum(step):
         return (part[step, tile] + part_in[step, 0]) + (part_in[step, 1] + part_in[step, 2])
 
-    def line_copies(buf, unit, send, recv, phase):
-        half = core * (SIDE * SIDE)
+    def to_ctx(ref, place, send_sem, recv_sem, to):
+        return pltpu.make_async_remote_copy(
+            src_ref=ref.at[place], dst_ref=ref.at[place], send_sem=send_sem, recv_sem=recv_sem,
+            device_id={"ctx": to}, device_id_type=MESH,
+        )
+
+    def gather(buf, step, between, late):
+        def along_minor(k):
+            return to_ctx(
+                buf, pl.ds(slot * 2, 2), a_send.at[step, k], a_recv.at[step, k], ctx_id(major, (minor + k) % SIDE)
+            )
+
+        def along_major(came, k):
+            place = pl.ds((half + major * SIDE + (minor + SIDE - came) % SIDE) * 2, 2)
+            return to_ctx(
+                buf, place, f_send.at[step, came, k], f_recv.at[step, came, k], ctx_id((major + k) % SIDE, minor)
+            )
+
+        def to_sibling(k):
+            place = pl.ds((half + (major + SIDE - k) % SIDE * SIDE) * 2, 2 * SIDE)
+            return to_ctx(buf, place, s_send.at[step, k], s_recv.at[step, k], sibling)
+
+        for k in NEAR_FIRST:
+            along_minor(k).start()
+        for k in NEAR_FIRST:
+            along_major(0, k).start()
+        between()
+
+        def forward(i, _):
+            came = near_first(i)
+            along_minor(came).wait_recv()
+            for k in NEAR_FIRST:
+                along_major(came, k).start()
+            return 0
+
+        lax.fori_loop(1, SIDE, forward, 0)
+        to_sibling(0).start()
+        late()
+
+        def arrive(i, _):
+            k = near_first(i)
+            for came in range(SIDE):
+                along_major(came, k).wait_recv()
+            to_sibling(k).start()
+            return 0
+
+        lax.fori_loop(1, SIDE, arrive, 0)
+        for k in range(SIDE):
+            to_sibling(k).wait()
+        for k in range(1, SIDE):
+            along_minor(k).wait_send()
+
+        def sent(k, _):
+            for came in range(SIDE):
+                along_major(came, k).wait_send()
+            return 0
+
+        lax.fori_loop(1, SIDE, sent, 0)
+
+    def ids_line(phase):
         copies = []
         for k in NEAR_FIRST:
             if phase == 0:
-                place = pl.ds((half + major * SIDE + minor) * unit, unit)
-                to = ctx_id(major, (minor + k) % SIDE)
+                place, to = pl.ds(slot, 1), ctx_id(major, (minor + k) % SIDE)
             else:
-                place = pl.ds((half + major * SIDE) * unit, SIDE * unit)
-                to = ctx_id((major + k) % SIDE, minor)
-            copies.append(
-                pltpu.make_async_remote_copy(
-                    src_ref=buf.at[place], dst_ref=buf.at[place],
-                    send_sem=send.at[phase, k], recv_sem=recv.at[phase, k],
-                    device_id={"ctx": to}, device_id_type=MESH,
-                )
-            )
+                place, to = pl.ds(half + major * SIDE, SIDE), ctx_id((major + k) % SIDE, minor)
+            copies.append(to_ctx(ids_all, place, i_send.at[phase, k], i_recv.at[phase, k], to))
         for c in copies:
             c.start()
         return copies
 
-    def sibling_copy(buf, unit, send, recv, k):
-        row = (major + SIDE - k) % SIDE
-        place = pl.ds((core * (SIDE * SIDE) + row * SIDE) * unit, SIDE * unit)
-        copy = pltpu.make_async_remote_copy(
-            src_ref=buf.at[place], dst_ref=buf.at[place],
-            send_sem=send.at[2, k], recv_sem=recv.at[2, k],
-            device_id={"ctx": sibling}, device_id_type=MESH,
-        )
-        copy.start()
-        return copy
-
-    def gather(bufs, between):
-        first = [line_copies(b, u, s, r, 0) for b, u, s, r in bufs]
-        between()
-        for f in first:
-            wait_all(f)
-        second = [line_copies(b, u, s, r, 1) for b, u, s, r in bufs]
-        third = [sibling_copy(b, u, s, r, 0) for b, u, s, r in bufs]
-        for i, k in enumerate(NEAR_FIRST):
-            for (b, u, s, r), copies in zip(bufs, second):
-                copies[i].wait()
-                third.append(sibling_copy(b, u, s, r, k))
-        wait_all(third)
-
     copies = tile_scatter(0)
+    ids_all[pl.ds(slot, 1)] = ids_v[...]
+    ids_first = ids_line(0)
 
     rates = turn_rates(tile)
     for p in range(PAIRS):
-        r = ids_s[0, PAIRS + 2 * p].astype(F32)
-        s = ids_s[0, PAIRS + 2 * p + 1].astype(F32)
-        phases[p] = cos_sin(rates, r, s)
+        phases[p] = cos_sin(rates, ids_s[0, 32 + p].astype(F32), ids_s[0, 64 + p].astype(F32))
     left64 = left_half((M, 2 * M))
+    loads[4].wait()
     for k in range(K):
         pk = pupils[k]
         turned = swap(pk)
         prr[k] = jnp.where(left64, pk, turned)
         pii[k] = jnp.where(left64, -turned, pk)
 
-    slot = core * (SIDE * SIDE) + major * SIDE + minor
     wait_all(copies)
     g1[pl.ds(slot * 2, 2)] = tile_sum(0).astype(BF16).reshape(2, Q, 2 * M)
-    ids_all[pl.ds(slot, 1)] = ids_v[...]
-    gather([(g1, 2, a_send.at[0], a_recv.at[0]), (ids_all, 1, i_send, i_recv)], lambda: None)
+    ids_second = []
+
+    def ids_on():
+        wait_all(ids_first)
+        ids_second.extend(ids_line(1))
+
+    def ids_end():
+        wait_all(ids_second)
+        copy = to_ctx(ids_all, pl.ds(half, SIDE * SIDE), i_send.at[2, 0], i_recv.at[2, 0], sibling)
+        copy.start()
+        ids_second[:] = [copy]
+
+    gather(g1, 0, ids_on, ids_end)
+    wait_all(ids_second)
 
     leftq = left_half((Q, 2 * M))
     for c in range(2):
@@ -241,11 +349,13 @@
         )
     for c in copies:
         c.start()
-    wait_all(copies)
-
+    for copy in loads[5:]:
+        copy.wait()
     fown = fst[:, own]
     fcat = jnp.concatenate([fown[:M], fown[M:]], 1)
-    gown = gcat[own, :]
+    gown = gown_v[...]
+    wait_all(copies)
+
     for c in range(2):
         s = jnp.concatenate([spec[t, c * Q : (c + 1) * Q] for t in range(T)], 0)
         s_sw = swap(s)
@@ -286,48 +396,28 @@
 
     wait_all(tile_scatter(1))
     g2[pl.ds(slot * 2, 2)] = tile_sum(1).astype(BF16).reshape(2, Q, 2 * M)
-    gather([(g2, 2, a_send.at[1], a_recv.at[1])], lambda: None)
-
-
-def pair_kernel(where_s, ids_s, ids_v, g2, out, lists_v, lists_s, acc, sem):
+
+    def make_lists():
+        for m, rows in enumerate(pair_lists(ids_all[...].reshape(CTX, 128), q)):
+            lists[m * 8 : (m + 1) * 8] = rows
+
+    gather(g2, 1, make_lists, lambda: None)
+
+
+def pair_kernel(where_s, lists_v, ids_v, g2, resist_v, out, resist, lists_s, ids_s, acc, sem, out_sem):
+    resist_copy = pltpu.make_async_copy(resist_v, resist, out_sem)
+    copy = pltpu.make_async_copy(lists_v, lists_s, sem)
+    copy.start()
+    resist_copy.start()
     me = where_s[0]
     rates = turn_rates(where_s[1])
-    ids = ids_v[...].reshape(CTX, 128)
-    lane = lax.broadcasted_iota(jnp.int32, (CTX, 128), 1)
-    sub = lax.broadcasted_iota(jnp.int32, (CTX, 128), 0)
-    sub8 = lax.broadcasted_iota(jnp.int32, (8, 128), 0)
-    lane8 = lax.broadcasted_iota(jnp.int32, (8, 128), 1)
-    weights = jnp.where(sub8 == 0, 1, jnp.where(sub8 == 1, lane8, 0)).astype(F32).astype(BF16)
-    before = jnp.where(sub < lane, 1.0, 0.0).astype(BF16)
-    for m in range(2):
-        match = jnp.where((ids == 2 * me + m) & (lane < PAIRS), 1.0, 0.0).astype(BF16)
-        stats = dot(weights, match, ((1,), (1,)))
-        count = jnp.broadcast_to(stats[0:1], (8, 128))
-        index = jnp.broadcast_to(stats[1:2], (8, 128))
-        single = jnp.where(count == 1.0, 1.0, 0.0)
-        rank = dot(single.astype(BF16), before)
-        hot = jnp.where(
-            (jnp.broadcast_to(rank[0:1], (CTX, 128)) == sub.astype(F32))
-            & (jnp.broadcast_to(single[0:1], (CTX, 128)) > 0.5),
-            1.0, 0.0,
-        ).astype(BF16)
-        load = jnp.where(sub8 == 0, lane8.astype(F32), jnp.where(sub8 == 1, index * single, jnp.where(sub8 == 2, 1.0, 0.0)))
-        listed = dot(load.astype(BF16), hot, ((1,), (1,)))
-        n_single = jnp.sum(single, axis=1, keepdims=True)
-        n_multi = jnp.sum(jnp.where(count > 1.5, 1.0, 0.0), axis=1, keepdims=True)
-        rows = jnp.where(sub8 == 3, n_single, jnp.where(sub8 == 4, n_multi, jnp.where(sub8 == 5, count, listed)))
-        lists_v[m * 8 : (m + 1) * 8] = rows.astype(jnp.int32)
-    copy = pltpu.make_async_copy(lists_v, lists_s, sem)
-    copy.start()
     copy.wait()
 
-    def terms(h, j, weight):
-        r = ids_s[h, 0, PAIRS + 2 * j].astype(F32)
-        s = ids_s[h, 0, PAIRS + 2 * j + 1].astype(F32)
-        g = g2[2 * h + j // SRC].astype(F32)
-        cs = cos_sin(rates, r, s)
+    def terms(context, r, s, weight):
+        g = g2[context].astype(F32)
+        cs = cos_sin(rates, r.astype(F32), s.astype(F32))
         if weight is not None:
-            cs = cs * weight
+            cs = cs * weight.astype(F32)
         return g * cs, swap(g) * cs
 
     block = 8
@@ -338,27 +428,29 @@
             sum_a, sum_b = carry
             for b in range(block):
                 k = i * block + b
-                add_a, add_b = terms(
-                    lists_s[m * 8, k], lists_s[m * 8 + 1, k], lists_s[m * 8 + 2, k].astype(F32)
-                )
+                add_a, add_b = terms(*[lists_s[m * 8 + row, k] for row in range(4)])
                 sum_a += add_a
                 sum_b += add_b
             return sum_a, sum_b
 
         zero = jnp.zeros((Q, 2 * M), F32)
-        sum_a, sum_b = lax.fori_loop(0, (lists_s[m * 8 + 3, 0] + block - 1) // block, step, (zero, zero))
+        sum_a, sum_b = lax.fori_loop(0, (lists_s[m * 8 + 4, 0] + block - 1) // block, step, (zero, zero))
         acc[0] = sum_a
         acc[1] = sum_b
 
-        @pl.when(lists_s[m * 8 + 4, 0] > 0)
+        @pl.when(lists_s[m * 8 + 5, 0] > 0)
         def _():
+            copy = pltpu.make_async_copy(ids_v, ids_s, sem)
+            copy.start()
+            copy.wait()
+
             def host(h, _):
-                @pl.when(lists_s[m * 8 + 5, h] > 1)
+                @pl.when(lists_s[m * 8 + 6, h] > 1)
                 def _():
                     def one(j, _):
                         @pl.when(ids_s[h, 0, j] == 2 * me + m)
                         def _():
-                            add_a, add_b = terms(h, j, None)
+                            add_a, add_b = terms(2 * h + j // SRC, ids_s[h, 0, 32 + j], ids_s[h, 0, 64 + j], None)
                             acc[0] += add_a
                             acc[1] += add_b
 
@@ -372,9 +464,10 @@
 
         sum_a, sum_b = acc[0], acc[1]
         out[m * Q : (m + 1) * Q] = jnp.where(left, sum_a - swap(sum_a), sum_b + swap(sum_b)).astype(BF16)
-
-
-def last_kernel(gq, p_st, q_st, out, rows, x_send, x_recv):
+    resist_copy.wait()
+
+
+def rows_kernel(gq, rows, x_send, x_recv):
     tile = lax.axis_index("tile")
     barrier = pltpu.get_barrier_semaphore()
     for k in range(1, T):
@@ -393,82 +486,125 @@
     for c in copies:
         c.start()
     wait_all(copies)
+
+
+def last_kernel(rows, p_st, q_st, out, held, sem):
     left = left_half((M, 2 * M))
+    copies = []
     for m in range(2):
         g = jnp.concatenate([rows[t, m * Q : (m + 1) * Q].astype(F32) for t in range(T)], 0)
         turned = swap(g)
         both = jnp.concatenate([g, jnp.where(left, turned, -turned)], 0).astype(BF16)
         lifted = dot(p_st[...], both, ((0,), (0,))).astype(BF16)
-        out[m] = dot(lifted, q_st[...])
+        held[m] = dot(lifted, q_st[...])
+        copies.append(pltpu.make_async_copy(held.at[m], out.at[m], sem.at[m]))
+        copies[-1].start()
+    wait_all(copies)
 
 
 def local(masks, blur_rows, blur_cols, pupils, targets, context_masters, offsets):
     vmem = pl.BlockSpec(memory_space=pltpu.VMEM)
     smem = pl.BlockSpec(memory_space=pltpu.SMEM)
+    hbm = pl.BlockSpec(memory_space=pltpu.HBM)
     dma = pltpu.SemaphoreType.DMA
+    stay = functools.partial(pltpu.with_memory_space_constraint, memory_space=pltpu.HBM)
+    gap = jnp.zeros((32 - PAIRS,), jnp.int32)
+    shifts = offsets.reshape(PAIRS, 2)
     packed = jnp.concatenate(
-        [context_masters.reshape(-1), offsets.reshape(-1), jnp.zeros((128 - 3 * PAIRS,), jnp.int32)]
+        [context_masters.reshape(-1), gap, shifts[:, 0], gap, shifts[:, 1], gap, jnp.zeros((32,), jnp.int32)]
     ).reshape(1, 128)
-    resist, g2, ids_all, p_st, q_st = pl.pallas_call(
+    resist_v, g2, ids_all, lists, p_st, q_st = pl.pallas_call(
         main_kernel,
         out_shape=(
             jax.ShapeDtypeStruct((2, R, N), BF16),
             jax.ShapeDtypeStruct((2 * CTX, Q, 2 * M), BF16),
             jax.ShapeDtypeStruct((CTX, 1, 128), jnp.int32),
+            jax.ShapeDtypeStruct((16, 128), jnp.int32),
             jax.ShapeDtypeStruct((2 * M, R), BF16),
             jax.ShapeDtypeStruct((2 * M, N), BF16),
         ),
-        in_specs=[vmem] * 5 + [smem] + [vmem] * 5,
-        out_specs=(vmem,) * 5,
+        in_specs=[hbm] * 5 + [smem, vmem] + [hbm] * 4,
+        out_specs=(vmem,) * 6,
         scratch_shapes=[
+            pltpu.VMEM((2, R, N), BF16),
+            pltpu.VMEM((N, R), BF16),
+            pltpu.VMEM((N, N), BF16),
+            pltpu.VMEM((K, M, 2 * M), F32),
+            pltpu.VMEM((2, R, N), BF16),
+            pltpu.VMEM((2 * M, N), BF16),
+            pltpu.VMEM((R, 2 * M), BF16),
+            pltpu.VMEM((2 * M, 2 * N), BF16),
+            pltpu.VMEM((2 * N, 4 * M), BF16),
             pltpu.VMEM((2 * CTX, Q, 2 * M), BF16),
             pltpu.VMEM((2, T, 2 * Q, 2 * M), F32),
             pltpu.VMEM((2, T - 1, 2 * Q, 2 * M), F32),
             pltpu.VMEM((T, 2 * Q, 2 * M), F32),
             pltpu.VMEM((K, M, 2 * M), F32),
             pltpu.VMEM((K, M, 2 * M), F32),
-            pltpu.VMEM((8, 128), F32),
             pltpu.VMEM((K * R, 2 * M), BF16),
             pltpu.VMEM((K * R, 2 * N), BF16),
             pltpu.VMEM((PAIRS, Q, 2 * M), F32),
+            dma((9,)),
             dma((3, T - 1)),
             dma((3, T - 1)),
-            dma((2, 3, SIDE)),
-            dma((2, 3, SIDE)),
+            dma((2, SIDE)),
+            dma((2, SIDE)),
+            dma((2, SIDE, SIDE)),
+            dma((2, SIDE, SIDE)),
+            dma((2, SIDE)),
+            dma((2, SIDE)),
             dma((3, SIDE)),
             dma((3, SIDE)),
         ],
         compiler_params=pltpu.CompilerParams(
-            collective_id=0, has_side_effects=True, vmem_limit_bytes=48 << 20
+            collective_id=0, has_side_effects=True, vmem_limit_bytes=40 << 20
         ),
         name="main",
-    )(masks, blur_rows, blur_cols, pupils, targets, packed, packed.reshape(1, 1, 128), *tables())
+    )(
+        *map(stay, (masks, blur_rows, blur_cols, pupils, targets)),
+        packed,
+        packed.reshape(1, 1, 128),
+        *map(stay, map(jnp.asarray, tables())),
+    )
     where = jnp.stack([lax.axis_index("ctx"), lax.axis_index("tile")]).astype(jnp.int32)
-    gq = pl.pallas_call(
+    gq, resist = pl.pallas_call(
         pair_kernel,
-        out_shape=jax.ShapeDtypeStruct((2 * Q, 2 * M), BF16),
-        in_specs=[smem, smem, vmem, vmem],
-        out_specs=vmem,
+        out_shape=(
+            jax.ShapeDtypeStruct((2 * Q, 2 * M), BF16),
+            jax.ShapeDtypeStruct((2, R, N), BF16),
+        ),
+        in_specs=[smem] + [vmem] * 4,
+        out_specs=(vmem, hbm),
         scratch_shapes=[
-            pltpu.VMEM((16, 128), jnp.int32),
             pltpu.SMEM((16, 128), jnp.int32),
+            pltpu.SMEM((CTX, 1, 128), jnp.int32),
             pltpu.VMEM((2, Q, 2 * M), F32),
+            dma,
             dma,
         ],
         compiler_params=pltpu.CompilerParams(vmem_limit_bytes=32 << 20),
         name="pairs",
-    )(where, ids_all, ids_all, g2)
+    )(where, lists, ids_all, g2, resist_v)
+    rows = pl.pallas_call(
+        rows_kernel,
+        out_shape=jax.ShapeDtypeStruct((T, 2 * Q, 2 * M), BF16),
+        in_specs=[vmem],
+        out_specs=vmem,
+        scratch_shapes=[dma((T - 1,)), dma((T - 1,))],
+        compiler_params=pltpu.CompilerParams(
+            collective_id=1, has_side_effects=True, vmem_limit_bytes=32 << 20
+        ),
+        name="rows",
+    )(gq)
     mask_grad = pl.pallas_call(
         last_kernel,
         out_shape=jax.ShapeDtypeStruct((2, R, N), F32),
         in_specs=[vmem] * 3,
-        out_specs=vmem,
-        scratch_shapes=[pltpu.VMEM((T, 2 * Q, 2 * M), BF16), dma((T - 1,)), dma((T - 1,))],
-        compiler_params=pltpu.CompilerParams(
-            collective_id=1, has_side_effects=True, vmem_limit_bytes=32 << 20
-        ),
+        out_specs=hbm,
+        scratch_shapes=[pltpu.VMEM((2, R, N), F32), dma((2,))],
+        compiler_params=pltpu.CompilerParams(vmem_limit_bytes=32 << 20),
         name="last",
-    )(gq, p_st, q_st)
+    )(rows, p_st, q_st)
     return (resist, mask_grad)
 
 

time: 86.1 us -> 70.8 us (0.82)
  the two profiles are of different devices: /device:TPU:16 before, /device:TPU:1 now
where the time goes in v2:
time: 70.8 us; the launch traced here: 70.4 us
  Pallas kernels  68.8 us (97%)
  local copies, waits for them, and re-layouts  0.85 us (1%)
    pallas_call x1, Pallas kernels, local(): pl.pallas_call(main_kernel, out_shape=(jax.ShapeDtypeStruct((2, R, N), BF...  61.2 us
    pallas_call x1, Pallas kernels, local(): pl.pallas_call(rows_kernel, out_shape=jax.ShapeDtypeStruct((T, 2 * Q, 2 *...  4.87 us

profile of v2, /device:TPU:1, one launch (start us, length us, event | category | flops | bytes accessed | tf_op | source)
XLA Modules:
  0.0 70.4 jit_solution(18285845209772803542)
XLA Ops:
  0.6 0.0 copy-start.1
  0.6 0.0 copy-start
  0.7 0.1 pad_add_fusion.where_s
  0.7 0.6 copy-done.1
  1.3 0.1 reshape.13
  1.4 0.0 copy-done
  1.4 0.1 reshape.14
  1.5 0.1 concatenate.3
  1.6 61.2 %main.1 = (bf16[2,128,512]{2,1,0:T(8,128)(2,1)S(1)}, bf16[256,16,128]{2,1,0:T(8,128)(2,1)S(1)}, s32[128,1,128]{2,1,0:T(1,128)S(1)}, s32[16,128]{1,0:T(8,128)S(1)...) custom-call(bf16[2,128,512]{2,1,0:T(8,128)(2,1)} %masks_h.1, bf16[512,512]{1,0:T(8,128)(2,1)} %br_h.1, ...), custom_call_target="tpu_custom_call" | custom-call | tf_op jit(solution)/shard_map/main/pallas_call | solution.py:516
  62.8 1.4 %pairs.1 = (bf16[32,128]{1,0:T(8,128)(2,1)S(1)}, bf16[2,128,512]{2,1,0:T(8,128)(2,1)}) custom-call(s32[2]{0:T(128)S(1)} %pad_add_fusion.where_s, s32[16,128]{1,0:T(8,128)S(1)} %get-tuple-element.10.lists_v, s32[128,1,128]{2,1,0:T(1,128)S(1)} %get-tuple-element.11.ids_v, bf16[256,16,128]{2,1,0:T(8,128)(2,1)S(1)} %get-tuple-element.12.g2, ...), custom_call_target="tpu_custom_call" | custom-call | tf_op jit(solution)/shard_map/pairs/pallas_call | solution.py:570
  64.2 4.9 %rows.1 = bf16[4,32,128]{2,1,0:T(8,128)(2,1)S(1)} custom-call(bf16[32,128]{1,0:T(8,128)(2,1)S(1)} %get-tuple-element.15.gq), custom_call_target="tpu_custom_call" | custom-call | tf_op jit(solution)/shard_map/rows/pallas_call | solution.py:588
  69.1 1.2 %last.1 = f32[2,128,512]{2,1,0:T(8,128)} custom-call(bf16[4,32,128]{2,1,0:T(8,128)(2,1)S(1)} %rows.1, bf16[128,128]{1,0:T(8,128)(2,1)S(1)} %get-tuple-element.16.p_st, bf16[128,512]{1,0:T(8,128)(2,1)S(1)} %get-tuple-element.17.q_st), custom_call_target="tpu_custom_call" | custom-call | tf_op jit(solution)/shard_map/last/pallas_call | solution.py:599
  (4 shorter events, 0.0 us)
Async XLA Ops:
  0.6 0.7 copy-start.1
  0.6 0.8 %copy-start = (s32[2,12,2]{1,2,0:T(2,128)S(1)}, s32[2,12,2]{1,2,0:T(2,128)}, u32[]{:S(2)}) copy-start(s32[2,12,2]{1,2,0:T(2,128)} %param.17) | copy-start | bytes 580

commit v3 on v2

--- a/solution.py
+++ b/solution.py
@@ -17,7 +17,8 @@
 K = 6
 T = 4
 R = N // T
-Q = M // T
+H = M // (2 * T)
+Q = 16
 SIDE = 8
 CTX = 2 * SIDE * SIDE
 SRC = 12
@@ -59,12 +60,84 @@
     return lax.broadcasted_iota(jnp.int32, shape, 1) < M
 
 
+def grid(shape):
+    return lax.broadcasted_iota(jnp.int32, shape, 0), lax.broadcasted_iota(jnp.int32, shape, 1)
+
+
 def turn_rates(tile):
-    row = lax.broadcasted_iota(jnp.int32, (Q, 2 * M), 0) + (tile * Q - M // 2)
-    lane = lax.broadcasted_iota(jnp.int32, (Q, 2 * M), 1)
-    col = lane % M - M // 2
+    row, lane = grid((Q, 2 * M))
+    v = lane % M
+    plain = row < H
+    early = v <= M // 2
+    f_u = jnp.where(plain, row + (tile * H - M // 2), jnp.where(early, 0, v - M // 2))
+    f_v = jnp.where(plain | early, v - M // 2, -(M // 2))
     late = jnp.where(lane < M, 0.0, 0.25).astype(F32)
-    return row.astype(F32) * (1.0 / N), col.astype(F32) * (1.0 / N), late
+    return f_u.astype(F32) * (1.0 / N), f_v.astype(F32) * (1.0 / N), late
+
+
+def from_rows(a):
+    row, lane = grid(a.shape)
+    real = jnp.where((lane == row + M // 2) & (row > 0), jnp.broadcast_to(a[:, 0:1], a.shape), 0.0)
+    imag = jnp.where((lane == row + M + M // 2) & (row > 0), jnp.broadcast_to(a[:, M : M + 1], a.shape), 0.0)
+    return jnp.sum(real + imag, axis=0, keepdims=True)
+
+
+def to_rows(e):
+    shape = (M // 2, 2 * M)
+    row, lane = grid(shape)
+    wide = jnp.broadcast_to(e, shape)
+    real = jnp.sum(jnp.where((lane == row + M // 2) & (row > 0), wide, 0.0), axis=1, keepdims=True)
+    imag = jnp.sum(jnp.where((lane == row + M + M // 2) & (row > 0), wide, 0.0), axis=1, keepdims=True)
+    first = jnp.where((row == 0) & (lane % M <= M // 2), wide, 0.0)
+    return first + jnp.where(lane == 0, real, 0.0) + jnp.where(lane == M, imag, 0.0)
+
+
+def exact(a, b):
+    return lax.dot_general(
+        a, b, (((1,), (0,)), ((), ())), precision=lax.Precision.HIGHEST, preferred_element_type=F32
+    )
+
+
+def mirrored(a):
+    src, dst = grid((2 * M, 2 * M))
+    both = jnp.where((src + dst == M) & (src < M) & (dst < M), 1.0, 0.0) - jnp.where((src + dst == 3 * M) & (src >= M), 1.0, 0.0)
+    return exact(a, both)
+
+
+def flipped(a):
+    row, col = grid((M // 2, M // 2))
+    return exact(jnp.where(row + col == M // 2, 1.0, 0.0), a)
+
+
+def expand(half, e):
+    row, lane = grid((M // 2, 2 * M))
+    e_mirrored = mirrored(jnp.broadcast_to(e, (8, 2 * M)))[0:1]
+    first = jnp.where((row == 0) & (lane % M > M // 2), jnp.broadcast_to(e_mirrored, row.shape), 0.0)
+    return jnp.concatenate([half, flipped(mirrored(half)) + first + to_rows(e)], 0)
+
+
+def fold(grad):
+    low = grad[M // 2 :]
+    turned = mirrored(low)
+    v = lax.broadcasted_iota(jnp.int32, (1, 2 * M), 1) % M
+    e = jnp.where(v <= M // 2, low[0:1], 0.0) + jnp.where((v > 0) & (v < M // 2), turned[0:1], 0.0)
+    return grad[: M // 2] + flipped(turned), e + from_rows(low)
+
+
+def half_of(spectrum):
+    low = spectrum[M // 2 :]
+    v = lax.broadcasted_iota(jnp.int32, (1, 2 * M), 1) % M
+    return spectrum[: M // 2], jnp.where(v <= M // 2, low[0:1], 0.0) + from_rows(low)
+
+
+def padded(e):
+    return jnp.where(lax.broadcasted_iota(jnp.int32, (Q - H, 2 * M), 0) == 0, jnp.broadcast_to(e, (Q - H, 2 * M)), 0.0)
+
+
+def pick(block, es, second):
+    return jnp.concatenate(
+        [jnp.where(second, block[H:], block[:H]), padded(jnp.where(second, es[1:2], es[0:1]))], 0
+    )
 
 
 def cos_sin(rates, r, s):
@@ -133,11 +206,11 @@
 
 
 def main_kernel(
-    masks_h, br_h, bc_h, pupils_h, targets_h, ids_s, ids_v, fst_h, gcat_h, inv_h, adj_h,
-    resist, g2, ids_all, lists, p_out, q_out,
+    masks_h, br_h, bc_h, pupils_h, targets_h, ids_h, shifts_h, fst_h, gcat_h, inv_h, adj_h,
+    resist, g2, e2, ids_all, lists, p_out, q_out,
     masks, br, bc, pupils, targets, fst, gown_v, inv, adj,
-    g1, part, part_in, spec, prr, pii, u_all, pull, phases,
-    load_sem, x_send, x_recv, a_send, a_recv, f_send, f_recv, s_send, s_recv, i_send, i_recv,
+    ids_s, shifts_s, g1, e1, part, part_in, spec, prr, pii, u_all, pull, phases,
+    load_sem, x_send, x_recv, a_send, a_recv, f_send, f_recv, s_send, s_recv, i_send, i_recv, e_send, e_recv,
 ):
     tile = lax.axis_index("tile")
     q = lax.axis_index("ctx")
@@ -161,6 +234,8 @@
                 (inv_h, inv),
                 (targets_h, targets),
                 (adj_h, adj),
+                (ids_h, ids_s),
+                (shifts_h, shifts_s),
             ]
         )
     ]
@@ -180,6 +255,11 @@
     for k in range(1, T):
         pl.semaphore_signal(barrier, inc=1, device_id={"tile": (tile + k) % T}, device_id_type=MESH)
     pl.semaphore_signal(barrier, inc=1, device_id={"ctx": sibling}, device_id_type=MESH)
+
+    def put(step, i, half_rows, e):
+        for t in range(T):
+            part[step, t, i * Q : i * Q + H] = half_rows[t * H : (t + 1) * H]
+            part[step, t, i * Q + H : (i + 1) * Q] = padded(e) if t == 0 else jnp.zeros((Q - H, 2 * M), F32)
 
     loads[0].wait()
     loads[1].wait()
@@ -195,8 +275,7 @@
     for m in range(2):
         a = dot(masks[m], qq, ((1,), (1,))).astype(BF16)
         s = dot(pcat, jnp.concatenate([a[:, : 2 * M], a[:, 2 * M :]], 0))
-        for t in range(T):
-            part[0, t, m * Q : (m + 1) * Q] = s[t * Q : (t + 1) * Q]
+        put(0, m, *half_of(s))
 
     pl.semaphore_wait(barrier, T - 1 + 2 * (SIDE - 1) + 1)
 
@@ -224,20 +303,20 @@
             device_id={"ctx": to}, device_id_type=MESH,
         )
 
-    def gather(buf, step, between, late):
+    def gather(buf, step, between, late, end):
         def along_minor(k):
             return to_ctx(
-                buf, pl.ds(slot * 2, 2), a_send.at[step, k], a_recv.at[step, k], ctx_id(major, (minor + k) % SIDE)
+                buf, pl.ds(slot, 1), a_send.at[step, k], a_recv.at[step, k], ctx_id(major, (minor + k) % SIDE)
             )
 
         def along_major(came, k):
-            place = pl.ds((half + major * SIDE + (minor + SIDE - came) % SIDE) * 2, 2)
+            place = pl.ds(half + major * SIDE + (minor + SIDE - came) % SIDE, 1)
             return to_ctx(
                 buf, place, f_send.at[step, came, k], f_recv.at[step, came, k], ctx_id((major + k) % SIDE, minor)
             )
 
         def to_sibling(k):
-            place = pl.ds((half + (major + SIDE - k) % SIDE * SIDE) * 2, 2 * SIDE)
+            place = pl.ds(half + (major + SIDE - k) % SIDE * SIDE, SIDE)
             return to_ctx(buf, place, s_send.at[step, k], s_recv.at[step, k], sibling)
 
         for k in NEAR_FIRST:
@@ -265,6 +344,7 @@
             return 0
 
         lax.fori_loop(1, SIDE, arrive, 0)
+        end()
         for k in range(SIDE):
             to_sibling(k).wait()
         for k in range(1, SIDE):
@@ -277,25 +357,67 @@
 
         lax.fori_loop(1, SIDE, sent, 0)
 
-    def ids_line(phase):
+    def line(buf, send, recv, phase):
         copies = []
-        for k in NEAR_FIRST:
-            if phase == 0:
-                place, to = pl.ds(slot, 1), ctx_id(major, (minor + k) % SIDE)
-            else:
-                place, to = pl.ds(half + major * SIDE, SIDE), ctx_id((major + k) % SIDE, minor)
-            copies.append(to_ctx(ids_all, place, i_send.at[phase, k], i_recv.at[phase, k], to))
+        if phase == 2:
+            copies.append(to_ctx(buf, pl.ds(half, SIDE * SIDE), send.at[2, 0], recv.at[2, 0], sibling))
+        else:
+            for k in NEAR_FIRST:
+                if phase == 0:
+                    place, to = pl.ds(slot, 1), ctx_id(major, (minor + k) % SIDE)
+                else:
+                    place, to = pl.ds(half + major * SIDE, SIDE), ctx_id((major + k) % SIDE, minor)
+                copies.append(to_ctx(buf, place, send.at[phase, k], recv.at[phase, k], to))
         for c in copies:
             c.start()
         return copies
 
+    def spread_out(step, buf, es):
+        total = tile_sum(step)
+        buf[pl.ds(slot, 1)] = jnp.concatenate([total[:H], total[Q : Q + H]], 0).astype(BF16).reshape(1, 2 * H, 2 * M)
+        es[pl.ds(slot, 1)] = jnp.concatenate([total[H : H + 1], total[Q + H : Q + H + 1]], 0).reshape(1, 2, 2 * M)
+        e_sems = (e_send.at[step], e_recv.at[step])
+        pending = []
+
+        def between():
+            pending.append(line(es, *e_sems, 0))
+            if step == 0:
+                wait_all(ids_copies.pop())
+                ids_copies.append(line(ids_all, i_send, i_recv, 1))
+            else:
+                for m, rows in enumerate(pair_lists(ids_all[...].reshape(CTX, 128), q)):
+                    lists[m * 8 : (m + 1) * 8] = rows
+
+        def late():
+            wait_all(pending.pop())
+            pending.append(line(es, *e_sems, 1))
+            if step == 0:
+                wait_all(ids_copies.pop())
+                ids_copies.append(line(ids_all, i_send, i_recv, 2))
+
+        def end():
+            wait_all(pending.pop())
+            pending.append(line(es, *e_sems, 2))
+
+        gather(buf, step, between, late, end)
+        wait_all(pending.pop())
+
     copies = tile_scatter(0)
-    ids_all[pl.ds(slot, 1)] = ids_v[...]
-    ids_first = ids_line(0)
+    loads[9].wait()
+    loads[10].wait()
+    lane = lax.broadcasted_iota(jnp.int32, (1, 128), 1)
+    own_ids = jnp.zeros((1, 128), jnp.int32)
+    for c in range(2):
+        for j in range(SRC):
+            for place, value in ((0, ids_s[c, j]), (32, shifts_s[c, 0, j]), (64, shifts_s[c, 1, j])):
+                own_ids = jnp.where(lane == place + c * SRC + j, value, own_ids)
+    ids_all[pl.ds(slot, 1)] = own_ids.reshape(1, 1, 128)
+    ids_copies = [line(ids_all, i_send, i_recv, 0)]
 
     rates = turn_rates(tile)
     for p in range(PAIRS):
-        phases[p] = cos_sin(rates, ids_s[0, 32 + p].astype(F32), ids_s[0, 64 + p].astype(F32))
+        c, j = p // SRC, p % SRC
+        phases[p] = cos_sin(rates, shifts_s[c, 0, j].astype(F32), shifts_s[c, 1, j].astype(F32))
     left64 = left_half((M, 2 * M))
     loads[4].wait()
     for k in range(K):
@@ -305,21 +427,8 @@
         pii[k] = jnp.where(left64, -turned, pk)
 
     wait_all(copies)
-    g1[pl.ds(slot * 2, 2)] = tile_sum(0).astype(BF16).reshape(2, Q, 2 * M)
-    ids_second = []
-
-    def ids_on():
-        wait_all(ids_first)
-        ids_second.extend(ids_line(1))
-
-    def ids_end():
-        wait_all(ids_second)
-        copy = to_ctx(ids_all, pl.ds(half, SIDE * SIDE), i_send.at[2, 0], i_recv.at[2, 0], sibling)
-        copy.start()
-        ids_second[:] = [copy]
-
-    gather(g1, 0, ids_on, ids_end)
-    wait_all(ids_second)
+    spread_out(0, g1, e1)
+    wait_all(ids_copies.pop())
 
     leftq = left_half((Q, 2 * M))
     for c in range(2):
@@ -327,13 +436,13 @@
         sum_b = jnp.zeros((Q, 2 * M), F32)
         for j in range(SRC):
             p = c * SRC + j
-            master = ids_s[0, p]
+            master = ids_s[c, j]
             owner = master >> 1
             ocore = owner & 1
             oy = (owner >> 1) & (SIDE - 1)
             oz = owner >> 4
             place = ocore * (SIDE * SIDE) + oz * SIDE + oy + ocore * (SIDE - 1) * (oy - oz)
-            g = g1[place * 2 + (master & 1)].astype(F32)
+            g = pick(g1[place].astype(F32), e1[place], (master & 1) > 0)
             cs = phases[p]
             sum_a += g * cs
             sum_b += swap(g) * cs
@@ -349,7 +458,7 @@
         )
     for c in copies:
         c.start()
-    for copy in loads[5:]:
+    for copy in loads[5:9]:
         copy.wait()
     fown = fst[:, own]
     fcat = jnp.concatenate([fown[:M], fown[M:]], 1)
@@ -357,7 +466,9 @@
     wait_all(copies)
 
     for c in range(2):
-        s = jnp.concatenate([spec[t, c * Q : (c + 1) * Q] for t in range(T)], 0)
+        s = expand(
+            jnp.concatenate([spec[t, c * Q : c * Q + H] for t in range(T)], 0), spec[0, c * Q + H : c * Q + H + 1]
+        )
         s_sw = swap(s)
         s2 = jnp.where(left64, -s_sw, s_sw)
         s2_sw = jnp.where(left64, s, -s)
@@ -391,30 +502,24 @@
             g_a += prr[k] * ga
             g_b += pii[k] * ga
         grad = g_a + swap(g_b)
-        for t in range(T):
-            part[1, t, c * Q : (c + 1) * Q] = grad[t * Q : (t + 1) * Q]
+        put(1, c, *fold(grad))
 
     wait_all(tile_scatter(1))
-    g2[pl.ds(slot * 2, 2)] = tile_sum(1).astype(BF16).reshape(2, Q, 2 * M)
-
-    def make_lists():
-        for m, rows in enumerate(pair_lists(ids_all[...].reshape(CTX, 128), q)):
-            lists[m * 8 : (m + 1) * 8] = rows
-
-    gather(g2, 1, make_lists, lambda: None)
-
-
-def pair_kernel(where_s, lists_v, ids_v, g2, resist_v, out, resist, lists_s, ids_s, acc, sem, out_sem):
+    spread_out(1, g2, e2)
+
+
+def pair_kernel(lists_v, ids_v, g2, e2, resist_v, out, resist, lists_s, ids_s, acc, sem, out_sem):
     resist_copy = pltpu.make_async_copy(resist_v, resist, out_sem)
     copy = pltpu.make_async_copy(lists_v, lists_s, sem)
     copy.start()
     resist_copy.start()
-    me = where_s[0]
-    rates = turn_rates(where_s[1])
+    me = lax.axis_index("ctx")
+    rates = turn_rates(lax.axis_index("tile"))
     copy.wait()
 
     def terms(context, r, s, weight):
-        g = g2[context].astype(F32)
+        host = context // 2
+        g = pick(g2[host].astype(F32), e2[host], context % 2 > 0)
         cs = cos_sin(rates, r.astype(F32), s.astype(F32))
         if weight is not None:
             cs = cs * weight.astype(F32)
@@ -492,7 +597,8 @@
     left = left_half((M, 2 * M))
     copies = []
     for m in range(2):
-        g = jnp.concatenate([rows[t, m * Q : (m + 1) * Q].astype(F32) for t in range(T)], 0)
+        parts = [rows[t].astype(F32)[m * Q : (m + 1) * Q] for t in range(T)]
+        g = jnp.concatenate([part[:H] for part in parts] + [to_rows(parts[0][H : H + 1])], 0)
         turned = swap(g)
         both = jnp.concatenate([g, jnp.where(left, turned, -turned)], 0).astype(BF16)
         lifted = dot(p_st[...], both, ((0,), (0,))).astype(BF16)
@@ -504,27 +610,22 @@
 
 def local(masks, blur_rows, blur_cols, pupils, targets, context_masters, offsets):
     vmem = pl.BlockSpec(memory_space=pltpu.VMEM)
-    smem = pl.BlockSpec(memory_space=pltpu.SMEM)
     hbm = pl.BlockSpec(memory_space=pltpu.HBM)
     dma = pltpu.SemaphoreType.DMA
     stay = functools.partial(pltpu.with_memory_space_constraint, memory_space=pltpu.HBM)
-    gap = jnp.zeros((32 - PAIRS,), jnp.int32)
-    shifts = offsets.reshape(PAIRS, 2)
-    packed = jnp.concatenate(
-        [context_masters.reshape(-1), gap, shifts[:, 0], gap, shifts[:, 1], gap, jnp.zeros((32,), jnp.int32)]
-    ).reshape(1, 128)
-    resist_v, g2, ids_all, lists, p_st, q_st = pl.pallas_call(
+    resist_v, g2, e2, ids_all, lists, p_st, q_st = pl.pallas_call(
         main_kernel,
         out_shape=(
             jax.ShapeDtypeStruct((2, R, N), BF16),
-            jax.ShapeDtypeStruct((2 * CTX, Q, 2 * M), BF16),
+            jax.ShapeDtypeStruct((CTX, 2 * H, 2 * M), BF16),
+            jax.ShapeDtypeStruct((CTX, 2, 2 * M), F32),
             jax.ShapeDtypeStruct((CTX, 1, 128), jnp.int32),
             jax.ShapeDtypeStruct((16, 128), jnp.int32),
             jax.ShapeDtypeStruct((2 * M, R), BF16),
             jax.ShapeDtypeStruct((2 * M, N), BF16),
         ),
-        in_specs=[hbm] * 5 + [smem, vmem] + [hbm] * 4,
-        out_specs=(vmem,) * 6,
+        in_specs=[hbm] * 11,
+        out_specs=(vmem,) * 7,
         scratch_shapes=[
             pltpu.VMEM((2, R, N), BF16),
             pltpu.VMEM((N, R), BF16),
@@ -535,7 +636,10 @@
             pltpu.VMEM((R, 2 * M), BF16),
             pltpu.VMEM((2 * M, 2 * N), BF16),
             pltpu.VMEM((2 * N, 4 * M), BF16),
-            pltpu.VMEM((2 * CTX, Q, 2 * M), BF16),
+            pltpu.SMEM((2, SRC), jnp.int32),
+            pltpu.SMEM((2, 2, SRC), jnp.int32),
+            pltpu.VMEM((CTX, 2 * H, 2 * M), BF16),
+            pltpu.VMEM((CTX, 2, 2 * M), F32),
             pltpu.VMEM((2, T, 2 * Q, 2 * M), F32),
             pltpu.VMEM((2, T - 1, 2 * Q, 2 * M), F32),
             pltpu.VMEM((T, 2 * Q, 2 * M), F32),
@@ -544,7 +648,7 @@
             pltpu.VMEM((K * R, 2 * M), BF16),
             pltpu.VMEM((K * R, 2 * N), BF16),
             pltpu.VMEM((PAIRS, Q, 2 * M), F32),
-            dma((9,)),
+            dma((11,)),
             dma((3, T - 1)),
             dma((3, T - 1)),
             dma((2, SIDE)),
@@ -555,6 +659,8 @@
             dma((2, SIDE)),
             dma((3, SIDE)),
             dma((3, SIDE)),
+            dma((2, 3, SIDE)),
+            dma((2, 3, SIDE)),
         ],
         compiler_params=pltpu.CompilerParams(
             collective_id=0, has_side_effects=True, vmem_limit_bytes=40 << 20
@@ -562,18 +668,17 @@
         name="main",
     )(
         *map(stay, (masks, blur_rows, blur_cols, pupils, targets)),
-        packed,
-        packed.reshape(1, 1, 128),
+        stay(context_masters),
+        stay(jnp.transpose(offsets, (0, 2, 1))),
         *map(stay, map(jnp.asarray, tables())),
     )
-    where = jnp.stack([lax.axis_index("ctx"), lax.axis_index("tile")]).astype(jnp.int32)
     gq, resist = pl.pallas_call(
         pair_kernel,
         out_shape=(
             jax.ShapeDtypeStruct((2 * Q, 2 * M), BF16),
             jax.ShapeDtypeStruct((2, R, N), BF16),
         ),
-        in_specs=[smem] + [vmem] * 4,
+        in_specs=[vmem] * 5,
         out_specs=(vmem, hbm),
         scratch_shapes=[
             pltpu.SMEM((16, 128), jnp.int32),
@@ -584,7 +689,7 @@
         ],
         compiler_params=pltpu.CompilerParams(vmem_limit_bytes=32 << 20),
         name="pairs",
-    )(where, lists, ids_all, g2, resist_v)
+    )(lists, ids_all, g2, e2, resist_v)
     rows = pl.pallas_call(
         rows_kernel,
         out_shape=jax.ShapeDtypeStruct((T, 2 * Q, 2 * M), BF16),

time: 70.8 us -> 68.8 us (0.972)
  Pallas kernels: 68.8 us -> 67.9 us
  local copies, waits for them, and re-layouts: 0.85 us -> 0 us
    pallas_call x1, Pallas kernels: 61.2 us -> 58.9 us  [local(): pl.pallas_call(main_kernel, out_shape=(jax.ShapeDtypeStruct((2, R, N), BF...]
    pallas_call x1, Pallas kernels: 1.4 us -> 2.81 us  [local(): pl.pallas_call(pair_kernel, out_shape=(jax.ShapeDtypeStruct((2 * Q, 2 * M...]
where the time goes in v3:
time: 68.8 us; the launch traced here: 68.6 us
  Pallas kernels  67.9 us (99%)
    pallas_call x1, Pallas kernels, local(): pl.pallas_call(main_kernel, out_shape=(jax.ShapeDtypeStruct((2, R, N), BF...  58.9 us
    pallas_call x1, Pallas kernels, local(): pl.pallas_call(rows_kernel, out_shape=jax.ShapeDtypeStruct((T, 2 * Q, 2 *...  4.87 us
    pallas_call x1, Pallas kernels, local(): pl.pallas_call(pair_kernel, out_shape=(jax.ShapeDtypeStruct((2 * Q, 2 * M...  2.81 us

profile of v3, /device:TPU:1, one launch (start us, length us, event | category | flops | bytes accessed | tf_op | source)
XLA Modules:
  0.0 68.6 jit_solution(7618677825305697985)
XLA Ops:
  0.6 58.9 %main.1 = (bf16[2,128,512]{2,1,0:T(8,128)(2,1)S(1)}, bf16[128,16,128]{2,1,0:T(8,128)(2,1)S(1)}, f32[128,2,128]{2,1,0:T(2,128)S(1)}, s32[128,1,128]{2,1,0:T(1,128...) custom-call(bf16[2,128,512]{2,1,0:T(8,128)(2,1)} %masks_h.1, ...), custom_call_target="tpu_custom_call" | custom-call | tf_op jit(solution)/shard_map/main/pallas_call | solution.py:616
  59.6 2.8 %pairs.1 = (bf16[32,128]{1,0:T(8,128)(2,1)S(1)}, bf16[2,128,512]{2,1,0:T(8,128)(2,1)}) custom-call(s32[16,128]{1,0:T(8,128)S(1)} %get-tuple-element.11.lists_v, s32[128,1,128]{2,1,0:T(1,128)S(1)} %get-tuple-element.12.ids_v, bf16[128,16,128]{2,1,0:T(8,128)(2,1)S(1)} %get-tuple-element.13.g2, f32[128,2,128]{2,1,0:T(2,128)S(1)} %get-tuple-element.14.e2, ...), custom_call_target="tpu_custom_call" | custom-call | tf_op jit(solution)/shard_map/pairs/pallas_call | solution.py:675
  62.4 4.9 %rows.1 = bf16[4,32,128]{2,1,0:T(8,128)(2,1)S(1)} custom-call(bf16[32,128]{1,0:T(8,128)(2,1)S(1)} %get-tuple-element.17.gq), custom_call_target="tpu_custom_call" | custom-call | tf_op jit(solution)/shard_map/rows/pallas_call | solution.py:693
  67.3 1.3 %last.1 = f32[2,128,512]{2,1,0:T(8,128)} custom-call(bf16[4,32,128]{2,1,0:T(8,128)(2,1)S(1)} %rows.1, bf16[128,128]{1,0:T(8,128)(2,1)S(1)} %get-tuple-element.18.p_st, bf16[128,512]{1,0:T(8,128)(2,1)S(1)} %get-tuple-element.19.q_st), custom_call_target="tpu_custom_call" | custom-call | tf_op jit(solution)/shard_map/last/pallas_call | solution.py:704

commit v4 on v3

--- a/solution.py
+++ b/solution.py
@@ -164,53 +164,45 @@
     return (i % 2) * ((i + 1) // 2) + (1 - i % 2) * (SIDE - i // 2)
 
 
-def pair_lists(ids, me):
-    lane = lax.broadcasted_iota(jnp.int32, (CTX, 128), 1)
-    sub = lax.broadcasted_iota(jnp.int32, (CTX, 128), 0)
-    sub8 = lax.broadcasted_iota(jnp.int32, (8, 128), 0)
-    lane8 = lax.broadcasted_iota(jnp.int32, (8, 128), 1).astype(F32)
+def pair_list(ids, me):
+    row, lane = grid((CTX, 128))
+    row8, lane8 = grid((8, 128))
     ones = jnp.full((8, 128), 1.0, BF16)
-    before = jnp.where(sub < lane, 1.0, 0.0).astype(BF16)
+    before = jnp.where(row < lane, 1.0, 0.0).astype(BF16)
     r = pltpu.roll(ids, 128 - 32, 1)
     s = pltpu.roll(ids, 128 - 64, 1)
-    second = jnp.where(lane >= SRC, 1.0, 0.0)
-    values = [second] + [v.astype(F32) for v in (r >> 4, r & 15, s >> 4, s & 15)]
-    lists = []
-    for m in range(2):
-        match = jnp.where((ids == 2 * me + m) & (lane < PAIRS), 1.0, 0.0)
-        count = dot(ones, match.astype(BF16), ((1,), (1,)))
-        found = [dot(ones, (match * v).astype(BF16), ((1,), (1,))) for v in values]
-        single = jnp.where(count == 1.0, 1.0, 0.0)
-        rank = dot(single.astype(BF16), before)
-        hot = jnp.where(
-            (jnp.broadcast_to(rank[0:1], (CTX, 128)) == sub.astype(F32))
-            & (jnp.broadcast_to(single[0:1], (CTX, 128)) > 0.5),
-            1.0, 0.0,
-        ).astype(BF16)
-        load = jnp.where(sub8 == 5, single, 0.0)
-        load = jnp.where(sub8 == 0, single * (2.0 * lane8 + found[0]), load)
-        for i in range(1, 5):
-            load = jnp.where(sub8 == i, single * found[i], load)
-        listed = dot(load.astype(BF16), hot, ((1,), (1,)))
-        line = [jnp.broadcast_to(listed[i : i + 1], (8, 128)) for i in range(6)]
-        n_single = jnp.sum(single, axis=1, keepdims=True)
-        n_multi = jnp.sum(jnp.where(count > 1.5, 1.0, 0.0), axis=1, keepdims=True)
-        rows = jnp.where(sub8 == 6, count, line[0])
-        rows = jnp.where(sub8 == 1, 16.0 * line[1] + line[2], rows)
-        rows = jnp.where(sub8 == 2, 16.0 * line[3] + line[4], rows)
-        rows = jnp.where(sub8 == 3, line[5], rows)
-        rows = jnp.where(sub8 == 4, n_single, rows)
-        rows = jnp.where(sub8 == 5, n_multi, rows)
-        lists.append(rows.astype(jnp.int32))
-    return lists
+    match = jnp.where((ids >> 1 == me) & (lane < PAIRS), 1.0, 0.0)
+    values = [jnp.where(lane >= SRC, 1.0, 0.0)] + [v.astype(F32) for v in (r >> 4, r & 15, s >> 4, s & 15, ids & 1)]
+    count = dot(ones, match.astype(BF16), ((1,), (1,)))
+    found = [dot(ones, (match * v).astype(BF16), ((1,), (1,))) for v in values]
+    single = jnp.where(count == 1.0, 1.0, 0.0)
+    rank = dot(single.astype(BF16), before)
+    hot = jnp.where(
+        (jnp.broadcast_to(rank[0:1], (CTX, 128)) == row.astype(F32))
+        & (jnp.broadcast_to(single[0:1], (CTX, 128)) > 0.5),
+        1.0, 0.0,
+    ).astype(BF16)
+    load = jnp.where(row8 == 6, single, 0.0)
+    load = jnp.where(row8 == 0, single * (2.0 * lane8.astype(F32) + found[0]), load)
+    for i in range(1, 6):
+        load = jnp.where(row8 == i, single * found[i], load)
+    listed = dot(load.astype(BF16), hot, ((1,), (1,)))
+    at = [jnp.broadcast_to(listed[i : i + 1], (8, 128)) for i in range(7)]
+    several = jnp.where(count > 1.5, 1.0, 0.0)
+    out = [at[0], 16.0 * at[1] + at[2], 16.0 * at[3] + at[4], at[6] - at[5], at[5]]
+    out += [jnp.broadcast_to(jnp.sum(several, axis=1, keepdims=True), (8, 128)), several]
+    rows = jnp.zeros((8, 128), F32)
+    for i, value in enumerate(out):
+        rows = jnp.where(row8 == i, value, rows)
+    return rows.astype(jnp.int32)
 
 
 def main_kernel(
     masks_h, br_h, bc_h, pupils_h, targets_h, ids_h, shifts_h, fst_h, gcat_h, inv_h, adj_h,
-    resist, g2, e2, ids_all, lists, p_out, q_out,
+    resist, g2, e2, ids_all, listed, p_out, q_out,
     masks, br, bc, pupils, targets, fst, gown_v, inv, adj,
     ids_s, shifts_s, g1, e1, part, part_in, spec, prr, pii, u_all, pull, phases,
-    load_sem, x_send, x_recv, a_send, a_recv, f_send, f_recv, s_send, s_recv, i_send, i_recv, e_send, e_recv,
+    load_sem, x_send, x_recv, g_send, a_recv, f_recv, s_send, s_recv, i_send, i_recv, e_send, e_recv,
 ):
     tile = lax.axis_index("tile")
     q = lax.axis_index("ctx")
@@ -303,74 +295,63 @@
             device_id={"ctx": to}, device_id_type=MESH,
         )
 
+    minor_ids = {k: ctx_id(major, (minor + k) % SIDE) for k in NEAR_FIRST}
+    major_ids = {k: ctx_id((major + k) % SIDE, minor) for k in NEAR_FIRST}
+    first = half + major * SIDE
+
     def gather(buf, step, between, late, end):
-        def along_minor(k):
-            return to_ctx(
-                buf, pl.ds(slot, 1), a_send.at[step, k], a_recv.at[step, k], ctx_id(major, (minor + k) % SIDE)
-            )
+        def along_minor(k, to):
+            return to_ctx(buf, pl.ds(slot, 1), g_send.at[step], a_recv.at[step, k], to)
 
         def along_major(came, k):
-            place = pl.ds(half + major * SIDE + (minor + SIDE - came) % SIDE, 1)
-            return to_ctx(
-                buf, place, f_send.at[step, came, k], f_recv.at[step, came, k], ctx_id((major + k) % SIDE, minor)
-            )
-
-        def to_sibling(k):
-            place = pl.ds(half + (major + SIDE - k) % SIDE * SIDE, SIDE)
-            return to_ctx(buf, place, s_send.at[step, k], s_recv.at[step, k], sibling)
+            place = pl.ds(first + (minor + SIDE - came) % SIDE, 1)
+            return to_ctx(buf, place, g_send.at[step], f_recv.at[step, k], major_ids[k])
+
+        def to_sibling(row):
+            return to_ctx(buf, pl.ds(half + row * SIDE, SIDE), s_send.at[step], s_recv.at[step], sibling)
+
+        def bytes_of(blocks, send_sem, recv_sem):
+            return to_ctx(buf, pl.ds(0, blocks), send_sem, recv_sem, sibling)
 
         for k in NEAR_FIRST:
-            along_minor(k).start()
+            along_minor(k, minor_ids[k]).start()
         for k in NEAR_FIRST:
             along_major(0, k).start()
         between()
 
         def forward(i, _):
             came = near_first(i)
-            along_minor(came).wait_recv()
+            along_minor(came, sibling).wait_recv()
             for k in NEAR_FIRST:
                 along_major(came, k).start()
             return 0
 
         lax.fori_loop(1, SIDE, forward, 0)
-        to_sibling(0).start()
+        to_sibling(major).start()
         late()
 
         def arrive(i, _):
             k = near_first(i)
-            for came in range(SIDE):
-                along_major(came, k).wait_recv()
-            to_sibling(k).start()
+            bytes_of(SIDE, g_send.at[step], f_recv.at[step, k]).wait_recv()
+            to_sibling((major + SIDE - k) % SIDE).start()
             return 0
 
         lax.fori_loop(1, SIDE, arrive, 0)
         end()
-        for k in range(SIDE):
-            to_sibling(k).wait()
-        for k in range(1, SIDE):
-            along_minor(k).wait_send()
-
-        def sent(k, _):
-            for came in range(SIDE):
-                along_major(came, k).wait_send()
-            return 0
-
-        lax.fori_loop(1, SIDE, sent, 0)
+        bytes_of((SIDE - 1) * (SIDE + 1), g_send.at[step], f_recv.at[step, 0]).wait_send()
+        bytes_of(SIDE * SIDE, s_send.at[step], s_recv.at[step]).wait()
 
     def line(buf, send, recv, phase):
-        copies = []
         if phase == 2:
-            copies.append(to_ctx(buf, pl.ds(half, SIDE * SIDE), send.at[2, 0], recv.at[2, 0], sibling))
+            places = [(pl.ds(half, SIDE * SIDE), sibling)]
+        elif phase == 1:
+            places = [(pl.ds(first, SIDE), major_ids[k]) for k in NEAR_FIRST]
         else:
-            for k in NEAR_FIRST:
-                if phase == 0:
-                    place, to = pl.ds(slot, 1), ctx_id(major, (minor + k) % SIDE)
-                else:
-                    place, to = pl.ds(half + major * SIDE, SIDE), ctx_id((major + k) % SIDE, minor)
-                copies.append(to_ctx(buf, place, send.at[phase, k], recv.at[phase, k], to))
-        for c in copies:
-            c.start()
-        return copies
+            places = [(pl.ds(slot, 1), minor_ids[k]) for k in NEAR_FIRST]
+        for place, to in places:
+            to_ctx(buf, place, send.at[phase], recv.at[phase], to).start()
+        blocks = (SIDE - 1, (SIDE - 1) * SIDE, SIDE * SIDE)[phase]
+        return [to_ctx(buf, pl.ds(0, blocks), send.at[phase], recv.at[phase], sibling)]
 
     def spread_out(step, buf, es):
         total = tile_sum(step)
@@ -385,8 +366,7 @@
                 wait_all(ids_copies.pop())
                 ids_copies.append(line(ids_all, i_send, i_recv, 1))
             else:
-                for m, rows in enumerate(pair_lists(ids_all[...].reshape(CTX, 128), q)):
-                    lists[m * 8 : (m + 1) * 8] = rows
+                listed[...] = pair_list(ids_all[...].reshape(CTX, 128), q)
 
         def late():
             wait_all(pending.pop())
@@ -508,76 +488,77 @@
     spread_out(1, g2, e2)
 
 
-def pair_kernel(lists_v, ids_v, g2, e2, resist_v, out, resist, lists_s, ids_s, acc, sem, out_sem):
-    resist_copy = pltpu.make_async_copy(resist_v, resist, out_sem)
-    copy = pltpu.make_async_copy(lists_v, lists_s, sem)
-    copy.start()
-    resist_copy.start()
+def pair_terms(g2, e2, rates, context, r, s):
+    host = context // 2
+    g = pick(g2[host].astype(F32), e2[host], context % 2 > 0)
+    cs = cos_sin(rates, r.astype(F32), s.astype(F32))
+    return g * cs, swap(g) * cs
+
+
+def several_kernel(list_v, ids_v, g2, e2, sums, list_s, ids_s, sems):
     me = lax.axis_index("ctx")
     rates = turn_rates(lax.axis_index("tile"))
-    copy.wait()
-
-    def terms(context, r, s, weight):
-        host = context // 2
-        g = pick(g2[host].astype(F32), e2[host], context % 2 > 0)
-        cs = cos_sin(rates, r.astype(F32), s.astype(F32))
-        if weight is not None:
-            cs = cs * weight.astype(F32)
-        return g * cs, swap(g) * cs
-
-    block = 8
-    left = left_half((Q, 2 * M))
-    for m in range(2):
-
-        def step(i, carry):
-            sum_a, sum_b = carry
-            for b in range(block):
-                k = i * block + b
-                add_a, add_b = terms(*[lists_s[m * 8 + row, k] for row in range(4)])
-                sum_a += add_a
-                sum_b += add_b
-            return sum_a, sum_b
-
-        zero = jnp.zeros((Q, 2 * M), F32)
-        sum_a, sum_b = lax.fori_loop(0, (lists_s[m * 8 + 4, 0] + block - 1) // block, step, (zero, zero))
-        acc[0] = sum_a
-        acc[1] = sum_b
-
-        @pl.when(lists_s[m * 8 + 5, 0] > 0)
-        def _():
-            copy = pltpu.make_async_copy(ids_v, ids_s, sem)
+    sums[...] = jnp.zeros_like(sums)
+
+    @pl.when(jnp.max(list_v[5:6, :]) > 0)
+    def _():
+        copies = [
+            pltpu.make_async_copy(list_v, list_s, sems.at[0]),
+            pltpu.make_async_copy(ids_v, ids_s, sems.at[1]),
+        ]
+        for copy in copies:
             copy.start()
-            copy.wait()
-
-            def host(h, _):
-                @pl.when(lists_s[m * 8 + 6, h] > 1)
-                def _():
-                    def one(j, _):
-                        @pl.when(ids_s[h, 0, j] == 2 * me + m)
-                        def _():
-                            add_a, add_b = terms(2 * h + j // SRC, ids_s[h, 0, 32 + j], ids_s[h, 0, 64 + j], None)
-                            acc[0] += add_a
-                            acc[1] += add_b
-
-                        return 0
-
-                    lax.fori_loop(0, PAIRS, one, 0)
-
-                return 0
-
-            lax.fori_loop(0, CTX, host, 0)
-
-        sum_a, sum_b = acc[0], acc[1]
-        out[m * Q : (m + 1) * Q] = jnp.where(left, sum_a - swap(sum_a), sum_b + swap(sum_b)).astype(BF16)
-    resist_copy.wait()
-
-
-def rows_kernel(gq, rows, x_send, x_recv):
+        wait_all(copies)
+
+        def host(h, _):
+            @pl.when(list_s[6, h] > 0)
+            def _():
+                def one(j, _):
+                    master = ids_s[h, 0, j]
+
+                    @pl.when(master >> 1 == me)
+                    def _():
+                        m = master & 1
+                        a, b = pair_terms(g2, e2, rates, 2 * h + j // SRC, ids_s[h, 0, 32 + j], ids_s[h, 0, 64 + j])
+                        sums[2 * m] += a
+                        sums[2 * m + 1] += b
+
+                    return 0
+
+                lax.fori_loop(0, PAIRS, one, 0)
+
+            return 0
+
+        lax.fori_loop(0, CTX, host, 0)
+
+
+def rows_kernel(list_v, g2, e2, sums, rows, list_s, sem, x_send, x_recv):
     tile = lax.axis_index("tile")
+    copy = pltpu.make_async_copy(list_v, list_s, sem)
+    copy.start()
     barrier = pltpu.get_barrier_semaphore()
     for k in range(1, T):
         pl.semaphore_signal(barrier, inc=1, device_id={"tile": (tile + k) % T}, device_id_type=MESH)
-    rows[tile] = gq[...]
+    rates = turn_rates(tile)
+    left = left_half((Q, 2 * M))
+    copy.wait()
+    block = 8
+
+    def step(i, carry):
+        total = list(carry)
+        for b in range(block):
+            k = i * block + b
+            a, b = pair_terms(g2, e2, rates, list_s[0, k], list_s[1, k], list_s[2, k])
+            for m in range(2):
+                weight = list_s[3 + m, k].astype(F32)
+                total[2 * m] += a * weight
+                total[2 * m + 1] += b * weight
+        return tuple(total)
+
+    total = lax.fori_loop(0, CTX // block, step, tuple(sums[i] for i in range(4)))
+    for m in range(2):
+        a, b = total[2 * m : 2 * m + 2]
+        rows[tile, m * Q : (m + 1) * Q] = jnp.where(left, a - swap(a), b + swap(b)).astype(BF16)
     pl.semaphore_wait(barrier, T - 1)
     copies = []
     for k in range(1, T):
@@ -593,9 +574,10 @@
     wait_all(copies)
 
 
-def last_kernel(rows, p_st, q_st, out, held, sem):
+def last_kernel(rows, p_st, q_st, resist_v, out, resist, held, sem):
     left = left_half((M, 2 * M))
-    copies = []
+    copies = [pltpu.make_async_copy(resist_v, resist, sem.at[2])]
+    copies[0].start()
     for m in range(2):
         parts = [rows[t].astype(F32)[m * Q : (m + 1) * Q] for t in range(T)]
         g = jnp.concatenate([part[:H] for part in parts] + [to_rows(parts[0][H : H + 1])], 0)
@@ -613,14 +595,14 @@
     hbm = pl.BlockSpec(memory_space=pltpu.HBM)
     dma = pltpu.SemaphoreType.DMA
     stay = functools.partial(pltpu.with_memory_space_constraint, memory_space=pltpu.HBM)
-    resist_v, g2, e2, ids_all, lists, p_st, q_st = pl.pallas_call(
+    resist_v, g2, e2, ids_all, listed, p_st, q_st = pl.pallas_call(
         main_kernel,
         out_shape=(
             jax.ShapeDtypeStruct((2, R, N), BF16),
             jax.ShapeDtypeStruct((CTX, 2 * H, 2 * M), BF16),
             jax.ShapeDtypeStruct((CTX, 2, 2 * M), F32),
             jax.ShapeDtypeStruct((CTX, 1, 128), jnp.int32),
-            jax.ShapeDtypeStruct((16, 128), jnp.int32),
+            jax.ShapeDtypeStruct((8, 128), jnp.int32),
             jax.ShapeDtypeStruct((2 * M, R), BF16),
             jax.ShapeDtypeStruct((2 * M, N), BF16),
         ),
@@ -651,16 +633,15 @@
             dma((11,)),
             dma((3, T - 1)),
             dma((3, T - 1)),
+            dma((2,)),
             dma((2, SIDE)),
             dma((2, SIDE)),
-            dma((2, SIDE, SIDE)),
-            dma((2, SIDE, SIDE)),
-            dma((2, SIDE)),
-            dma((2, SIDE)),
-            dma((3, SIDE)),
-            dma((3, SIDE)),
-            dma((2, 3, SIDE)),
-            dma((2, 3, SIDE)),
+            dma((2,)),
+            dma((2,)),
+            dma((3,)),
+            dma((3,)),
+            dma((2, 3)),
+            dma((2, 3)),
         ],
         compiler_params=pltpu.CompilerParams(
             collective_id=0, has_side_effects=True, vmem_limit_bytes=40 << 20
@@ -672,44 +653,42 @@
         stay(jnp.transpose(offsets, (0, 2, 1))),
         *map(stay, map(jnp.asarray, tables())),
     )
-    gq, resist = pl.pallas_call(
-        pair_kernel,
-        out_shape=(
-            jax.ShapeDtypeStruct((2 * Q, 2 * M), BF16),
-            jax.ShapeDtypeStruct((2, R, N), BF16),
-        ),
-        in_specs=[vmem] * 5,
-        out_specs=(vmem, hbm),
+    sums = pl.pallas_call(
+        several_kernel,
+        out_shape=jax.ShapeDtypeStruct((4, Q, 2 * M), F32),
+        in_specs=[vmem] * 4,
+        out_specs=vmem,
         scratch_shapes=[
-            pltpu.SMEM((16, 128), jnp.int32),
+            pltpu.SMEM((8, 128), jnp.int32),
             pltpu.SMEM((CTX, 1, 128), jnp.int32),
-            pltpu.VMEM((2, Q, 2 * M), F32),
-            dma,
-            dma,
+            dma((2,)),
         ],
         compiler_params=pltpu.CompilerParams(vmem_limit_bytes=32 << 20),
-        name="pairs",
-    )(lists, ids_all, g2, e2, resist_v)
+        name="several",
+    )(listed, ids_all, g2, e2)
     rows = pl.pallas_call(
         rows_kernel,
         out_shape=jax.ShapeDtypeStruct((T, 2 * Q, 2 * M), BF16),
-        in_specs=[vmem],
+        in_specs=[vmem] * 4,
         out_specs=vmem,
-        scratch_shapes=[dma((T - 1,)), dma((T - 1,))],
+        scratch_shapes=[pltpu.SMEM((8, 128), jnp.int32), dma, dma((T - 1,)), dma((T - 1,))],
         compiler_params=pltpu.CompilerParams(
             collective_id=1, has_side_effects=True, vmem_limit_bytes=32 << 20
         ),
         name="rows",
-    )(gq)
-    mask_grad = pl.pallas_call(
+    )(listed, g2, e2, sums)
+    mask_grad, resist = pl.pallas_call(
         last_kernel,
-        out_shape=jax.ShapeDtypeStruct((2, R, N), F32),
-        in_specs=[vmem] * 3,
-        out_specs=hbm,
-        scratch_shapes=[pltpu.VMEM((2, R, N), F32), dma((2,))],
+        out_shape=(
+            jax.ShapeDtypeStruct((2, R, N), F32),
+            jax.ShapeDtypeStruct((2, R, N), BF16),
+        ),
+        in_specs=[vmem] * 4,
+        out_specs=(hbm, hbm),
+        scratch_shapes=[pltpu.VMEM((2, R, N), F32), dma((3,))],
         compiler_params=pltpu.CompilerParams(vmem_limit_bytes=32 << 20),
         name="last",
-    )(rows, p_st, q_st)
+    )(rows, p_st, q_st, resist_v)
     return (resist, mask_grad)
 
 

time: 68.8 us -> 63.9 us (0.929)
  Pallas kernels: 67.9 us -> 63.1 us
    pallas_call x1, Pallas kernels: 58.9 us -> 55.2 us  [local(): pl.pallas_call(main_kernel, out_shape=(jax.ShapeDtypeStruct((2, R, N), BF...]
    pallas_call x2, Pallas kernels: 4.13 us -> 1.55 us  [the longest x1 1.33 us: local(): pl.pallas_call(last_kernel, out_shape=(jax.ShapeDtypeStruct((2, R, N), F3...]
    pallas_call x1, Pallas kernels: 4.87 us -> 6.32 us  [local(): pl.pallas_call(rows_kernel, out_shape=jax.ShapeDtypeStruct((T, 2 * Q, 2 *...]
where the time goes in v4:
time: 63.9 us; the launch traced here: 63.8 us
  Pallas kernels  63.1 us (99%)
  between operations  0.66 us (1%)
    pallas_call x1, Pallas kernels, local(): pl.pallas_call(main_kernel, out_shape=(jax.ShapeDtypeStruct((2, R, N), BF...  55.2 us
    pallas_call x1, Pallas kernels, local(): pl.pallas_call(rows_kernel, out_shape=jax.ShapeDtypeStruct((T, 2 * Q, 2 *...  6.32 us
    pallas_call x1, Pallas kernels, local(): pl.pallas_call(last_kernel, out_shape=(jax.ShapeDtypeStruct((2, R, N), F3...  1.33 us

profile of v4, /device:TPU:1, one launch (start us, length us, event | category | flops | bytes accessed | tf_op | source)
XLA Modules:
  0.0 63.8 jit_solution(9160335568146894762)
XLA Ops:
  0.6 55.2 %main.1 = (bf16[2,128,512]{2,1,0:T(8,128)(2,1)S(1)}, bf16[128,16,128]{2,1,0:T(8,128)(2,1)S(1)}, f32[128,2,128]{2,1,0:T(2,128)S(1)}, s32[128,1,128]{2,1,0:T(1,128...) custom-call(bf16[2,128,512]{2,1,0:T(8,128)(2,1)} %masks_h.1, ...), custom_call_target="tpu_custom_call" | custom-call | tf_op jit(solution)/shard_map/main/pallas_call | solution.py:598
  55.9 0.2 several.1.sums
  56.1 6.3 %rows.1 = bf16[4,32,128]{2,1,0:T(8,128)(2,1)S(1)} custom-call(s32[8,128]{1,0:T(8,128)S(1)} %get-tuple-element.11.list_v, bf16[128,16,128]{2,1,0:T(8,128)(2,1)S(1)} %get-tuple-element.12.g2, f32[128,2,128]{2,1,0:T(2,128)S(1)} %get-tuple-element.13.e2, f32[4,16,128]{2,1,0:T(8,128)S(1)} %several.1.sums), custom_call_target="tpu_custom_call" | custom-call | tf_op jit(solution)/shard_map/rows/pallas_call | solution.py:669
  62.4 1.3 %last.1 = (f32[2,128,512]{2,1,0:T(8,128)}, bf16[2,128,512]{2,1,0:T(8,128)(2,1)}) custom-call(bf16[4,32,128]{2,1,0:T(8,128)(2,1)S(1)} %rows.1, bf16[128,128]{1,0:T(8,128)(2,1)S(1)} %get-tuple-element.15.p_st, bf16[128,512]{1,0:T(8,128)(2,1)S(1)} %get-tuple-element.16.q_st, bf16[2,128,512]{2,1,0:T(8,128)(2,1)S(1)} %get-tuple-element.17.resist_v), custom_call_target="tpu_custom_call" | custom-call | tf_op jit(solution)/shard_map/last/pallas_call | solution.py:680

commit v5 on v4

--- a/solution.py
+++ b/solution.py
@@ -92,36 +92,51 @@
     return first + jnp.where(lane == 0, real, 0.0) + jnp.where(lane == M, imag, 0.0)
 
 
-def exact(a, b):
-    return lax.dot_general(
-        a, b, (((1,), (0,)), ((), ())), precision=lax.Precision.HIGHEST, preferred_element_type=F32
-    )
+def split(a):
+    high = a.astype(BF16)
+    return high, (a - high.astype(F32)).astype(BF16)
 
 
 def mirrored(a):
     src, dst = grid((2 * M, 2 * M))
-    both = jnp.where((src + dst == M) & (src < M) & (dst < M), 1.0, 0.0) - jnp.where((src + dst == 3 * M) & (src >= M), 1.0, 0.0)
-    return exact(a, both)
-
-
-def flipped(a):
+    real = jnp.where((src + dst == M) & (src < M) & (dst < M), 1.0, 0.0)
+    both = real - jnp.where((src + dst == 3 * M) & (src >= M), 1.0, 0.0)
+    out = dot(jnp.concatenate(split(a), 0), both.astype(BF16))
+    return out[: a.shape[0]] + out[a.shape[0] :]
+
+
+def flipped(blocks):
     row, col = grid((M // 2, M // 2))
-    return exact(jnp.where(row + col == M // 2, 1.0, 0.0), a)
-
-
-def expand(half, e):
+    turn = jnp.where(row + col == M // 2, 1.0, 0.0).astype(BF16)
+    out = dot(turn, jnp.concatenate([part for a in blocks for part in split(a)], 1))
+    part = [out[:, i * 2 * M : (i + 1) * 2 * M] for i in range(2 * len(blocks))]
+    return [part[2 * i] + part[2 * i + 1] for i in range(len(blocks))]
+
+
+def expand(halves, es):
     row, lane = grid((M // 2, 2 * M))
-    e_mirrored = mirrored(jnp.broadcast_to(e, (8, 2 * M)))[0:1]
-    first = jnp.where((row == 0) & (lane % M > M // 2), jnp.broadcast_to(e_mirrored, row.shape), 0.0)
-    return jnp.concatenate([half, flipped(mirrored(half)) + first + to_rows(e)], 0)
-
-
-def fold(grad):
-    low = grad[M // 2 :]
-    turned = mirrored(low)
+    wide = [jnp.broadcast_to(e, (16, 2 * M)) for e in es]
+    turned = mirrored(jnp.concatenate([*halves, *wide], 0))
+    lower = flipped([turned[: M // 2], turned[M // 2 : M]])
+    out = []
+    for i in range(2):
+        e_turned = jnp.broadcast_to(turned[M + 16 * i : M + 16 * i + 1], row.shape)
+        first = jnp.where((row == 0) & (lane % M > M // 2), e_turned, 0.0)
+        out.append(jnp.concatenate([halves[i], lower[i] + first + to_rows(es[i])], 0))
+    return out
+
+
+def fold(grads):
+    low = [grad[M // 2 :] for grad in grads]
+    turned = mirrored(jnp.concatenate(low, 0))
+    upper = flipped([turned[: M // 2], turned[M // 2 :]])
     v = lax.broadcasted_iota(jnp.int32, (1, 2 * M), 1) % M
-    e = jnp.where(v <= M // 2, low[0:1], 0.0) + jnp.where((v > 0) & (v < M // 2), turned[0:1], 0.0)
-    return grad[: M // 2] + flipped(turned), e + from_rows(low)
+    out = []
+    for i in range(2):
+        t = turned[i * (M // 2) : i * (M // 2) + 1]
+        e = jnp.where(v <= M // 2, low[i][0:1], 0.0) + jnp.where((v > 0) & (v < M // 2), t, 0.0)
+        out.append((grads[i][: M // 2] + upper[i], e + from_rows(low[i])))
+    return out
 
 
 def half_of(spectrum):
@@ -199,10 +214,10 @@
 
 def main_kernel(
     masks_h, br_h, bc_h, pupils_h, targets_h, ids_h, shifts_h, fst_h, gcat_h, inv_h, adj_h,
-    resist, g2, e2, ids_all, listed, p_out, q_out,
+    resist, g2, e2, ids_all, listed, pair_cs, p_out, q_out,
     masks, br, bc, pupils, targets, fst, gown_v, inv, adj,
-    ids_s, shifts_s, g1, e1, part, part_in, spec, prr, pii, u_all, pull, phases,
-    load_sem, x_send, x_recv, g_send, a_recv, f_recv, s_send, s_recv, i_send, i_recv, e_send, e_recv,
+    ids_s, shifts_s, list_s, g1, e1, part, part_in, spec, prr, pii, u_all, pull, phases,
+    load_sem, list_sem, x_send, x_recv, g_send, a_recv, f_recv, s_send, s_recv, i_send, i_recv, e_send, e_recv,
 ):
     tile = lax.axis_index("tile")
     q = lax.axis_index("ctx")
@@ -365,8 +380,6 @@
             if step == 0:
                 wait_all(ids_copies.pop())
                 ids_copies.append(line(ids_all, i_send, i_recv, 1))
-            else:
-                listed[...] = pair_list(ids_all[...].reshape(CTX, 128), q)
 
         def late():
             wait_all(pending.pop())
@@ -438,6 +451,9 @@
         )
     for c in copies:
         c.start()
+    listed[...] = pair_list(ids_all[...].reshape(CTX, 128), q)
+    list_copy = pltpu.make_async_copy(listed, list_s, list_sem)
+    list_copy.start()
     for copy in loads[5:9]:
         copy.wait()
     fown = fst[:, own]
@@ -445,10 +461,10 @@
     gown = gown_v[...]
     wait_all(copies)
 
+    halves = [jnp.concatenate([spec[t, c * Q : c * Q + H] for t in range(T)], 0) for c in range(2)]
+    spectra = expand(halves, [spec[0, c * Q + H : c * Q + H + 1] for c in range(2)])
     for c in range(2):
-        s = expand(
-            jnp.concatenate([spec[t, c * Q : c * Q + H] for t in range(T)], 0), spec[0, c * Q + H : c * Q + H + 1]
-        )
+        s = spectra[c]
         s_sw = swap(s)
         s2 = jnp.where(left64, -s_sw, s_sw)
         s2_sw = jnp.where(left64, s, -s)
@@ -456,24 +472,31 @@
             a1 = prr[k] * s + pii[k] * s_sw
             a2 = prr[k] * s2 + pii[k] * s2_sw
             both = jnp.concatenate([a1, a2], 0).astype(BF16)
-            u_all[k * R : (k + 1) * R] = dot(gown, both).astype(BF16)
-        for b in range(T):
-            cols = slice(b * R, (b + 1) * R)
-            field = dot(u_all[...], inv[:, b * 2 * R : (b + 1) * 2 * R])
-            intensity = jnp.zeros((R, R), F32)
-            for k in range(K):
-                fr = field[k * R : (k + 1) * R, :R]
-                fi = field[k * R : (k + 1) * R, R:]
-                intensity += fr * fr + fi * fi
-            image = 1.0 / (1.0 + jnp.exp(-STEEPNESS * (intensity - THRESHOLD)))
-            resist[c, :, cols] = image.astype(BF16)
-            slope = (image - targets[c, :, cols].astype(F32)) * (2.0 * STEEPNESS) * image * (1.0 - image)
-            slope2 = jnp.concatenate([slope, slope], 1)
-            for k in range(K):
-                pull[k * R : (k + 1) * R, b * 2 * R : (b + 1) * 2 * R] = (
-                    slope2 * field[k * R : (k + 1) * R]
-                ).astype(BF16)
-        folded = dot(pull[...], adj[...]).astype(BF16)
+            u_all[c, k * R : (k + 1) * R] = dot(gown, both).astype(BF16)
+
+    def field_of(i):
+        c, b = i // T, i % T
+        return dot(u_all[c], inv[:, b * 2 * R : (b + 1) * 2 * R])
+
+    def use(i, field):
+        c, b = i // T, i % T
+        cols = slice(b * R, (b + 1) * R)
+        intensity = jnp.zeros((R, R), F32)
+        for k in range(K):
+            fr = field[k * R : (k + 1) * R, :R]
+            fi = field[k * R : (k + 1) * R, R:]
+            intensity += fr * fr + fi * fi
+        image = 1.0 / (1.0 + jnp.exp(-STEEPNESS * (intensity - THRESHOLD)))
+        resist[c, :, cols] = image.astype(BF16)
+        slope = (image - targets[c, :, cols].astype(F32)) * (2.0 * STEEPNESS) * image * (1.0 - image)
+        slope2 = jnp.concatenate([slope, slope], 1)
+        for k in range(K):
+            pull[c, k * R : (k + 1) * R, b * 2 * R : (b + 1) * 2 * R] = (
+                slope2 * field[k * R : (k + 1) * R]
+            ).astype(BF16)
+
+    def gradient(c):
+        folded = dot(pull[c], adj[...]).astype(BF16)
         g_a = jnp.zeros((M, 2 * M), F32)
         g_b = jnp.zeros((M, 2 * M), F32)
         for k in range(K):
@@ -481,17 +504,37 @@
             ga = dot(fcat, jnp.concatenate([fk[:, : 2 * M], fk[:, 2 * M :]], 0))
             g_a += prr[k] * ga
             g_b += pii[k] * ga
-        grad = g_a + swap(g_b)
-        put(1, c, *fold(grad))
-
-    wait_all(tile_scatter(1))
+        return g_a + swap(g_b)
+
+    grads = []
+    coming = field_of(0)
+    for i in range(2 * T):
+        field = coming
+        if i < 2 * T - 1:
+            coming = field_of(i + 1)
+        use(i, field)
+        if i % T == T - 1:
+            grads.append(gradient(i // T))
+    for c, (half_rows, e) in enumerate(fold(grads)):
+        put(1, c, half_rows, e)
+
+    copies = tile_scatter(1)
+    list_copy.wait()
+
+    def pair_phases(i, _):
+        for b in range(8):
+            k = i * 8 + b
+            pair_cs[k] = cos_sin(rates, list_s[1, k].astype(F32), list_s[2, k].astype(F32))
+        return 0
+
+    lax.fori_loop(0, CTX // 8, pair_phases, 0)
+    wait_all(copies)
     spread_out(1, g2, e2)
 
 
-def pair_terms(g2, e2, rates, context, r, s):
+def pair_terms(g2, e2, context, cs):
     host = context // 2
     g = pick(g2[host].astype(F32), e2[host], context % 2 > 0)
-    cs = cos_sin(rates, r.astype(F32), s.astype(F32))
     return g * cs, swap(g) * cs
 
 
@@ -519,7 +562,8 @@
                     @pl.when(master >> 1 == me)
                     def _():
                         m = master & 1
-                        a, b = pair_terms(g2, e2, rates, 2 * h + j // SRC, ids_s[h, 0, 32 + j], ids_s[h, 0, 64 + j])
+                        cs = cos_sin(rates, ids_s[h, 0, 32 + j].astype(F32), ids_s[h, 0, 64 + j].astype(F32))
+                        a, b = pair_terms(g2, e2, 2 * h + j // SRC, cs)
                         sums[2 * m] += a
                         sums[2 * m + 1] += b
 
@@ -532,14 +576,13 @@
         lax.fori_loop(0, CTX, host, 0)
 
 
-def rows_kernel(list_v, g2, e2, sums, rows, list_s, sem, x_send, x_recv):
+def rows_kernel(list_v, pair_cs, g2, e2, sums, rows, list_s, sem, x_send, x_recv):
     tile = lax.axis_index("tile")
     copy = pltpu.make_async_copy(list_v, list_s, sem)
     copy.start()
     barrier = pltpu.get_barrier_semaphore()
     for k in range(1, T):
         pl.semaphore_signal(barrier, inc=1, device_id={"tile": (tile + k) % T}, device_id_type=MESH)
-    rates = turn_rates(tile)
     left = left_half((Q, 2 * M))
     copy.wait()
     block = 8
@@ -548,7 +591,7 @@
         total = list(carry)
         for b in range(block):
             k = i * block + b
-            a, b = pair_terms(g2, e2, rates, list_s[0, k], list_s[1, k], list_s[2, k])
+            a, b = pair_terms(g2, e2, list_s[0, k], pair_cs[k])
             for m in range(2):
                 weight = list_s[3 + m, k].astype(F32)
                 total[2 * m] += a * weight
@@ -595,7 +638,7 @@
     hbm = pl.BlockSpec(memory_space=pltpu.HBM)
     dma = pltpu.SemaphoreType.DMA
     stay = functools.partial(pltpu.with_memory_space_constraint, memory_space=pltpu.HBM)
-    resist_v, g2, e2, ids_all, listed, p_st, q_st = pl.pallas_call(
+    resist_v, g2, e2, ids_all, listed, pair_cs, p_st, q_st = pl.pallas_call(
         main_kernel,
         out_shape=(
             jax.ShapeDtypeStruct((2, R, N), BF16),
@@ -603,11 +646,12 @@
             jax.ShapeDtypeStruct((CTX, 2, 2 * M), F32),
             jax.ShapeDtypeStruct((CTX, 1, 128), jnp.int32),
             jax.ShapeDtypeStruct((8, 128), jnp.int32),
+            jax.ShapeDtypeStruct((CTX, Q, 2 * M), F32),
             jax.ShapeDtypeStruct((2 * M, R), BF16),
             jax.ShapeDtypeStruct((2 * M, N), BF16),
         ),
         in_specs=[hbm] * 11,
-        out_specs=(vmem,) * 7,
+        out_specs=(vmem,) * 8,
         scratch_shapes=[
             pltpu.VMEM((2, R, N), BF16),
             pltpu.VMEM((N, R), BF16),
@@ -620,6 +664,7 @@
             pltpu.VMEM((2 * N, 4 * M), BF16),
             pltpu.SMEM((2, SRC), jnp.int32),
             pltpu.SMEM((2, 2, SRC), jnp.int32),
+            pltpu.SMEM((8, 128), jnp.int32),
             pltpu.VMEM((CTX, 2 * H, 2 * M), BF16),
             pltpu.VMEM((CTX, 2, 2 * M), F32),
             pltpu.VMEM((2, T, 2 * Q, 2 * M), F32),
@@ -627,10 +672,11 @@
             pltpu.VMEM((T, 2 * Q, 2 * M), F32),
             pltpu.VMEM((K, M, 2 * M), F32),
             pltpu.VMEM((K, M, 2 * M), F32),
-            pltpu.VMEM((K * R, 2 * M), BF16),
-            pltpu.VMEM((K * R, 2 * N), BF16),
+            pltpu.VMEM((2, K * R, 2 * M), BF16),
+            pltpu.VMEM((2, K * R, 2 * N), BF16),
             pltpu.VMEM((PAIRS, Q, 2 * M), F32),
             dma((11,)),
+            dma,
             dma((3, T - 1)),
             dma((3, T - 1)),
             dma((2,)),
@@ -669,14 +715,14 @@
     rows = pl.pallas_call(
         rows_kernel,
         out_shape=jax.ShapeDtypeStruct((T, 2 * Q, 2 * M), BF16),
-        in_specs=[vmem] * 4,
+        in_specs=[vmem] * 5,
         out_specs=vmem,
         scratch_shapes=[pltpu.SMEM((8, 128), jnp.int32), dma, dma((T - 1,)), dma((T - 1,))],
         compiler_params=pltpu.CompilerParams(
             collective_id=1, has_side_effects=True, vmem_limit_bytes=32 << 20
         ),
         name="rows",
-    )(listed, g2, e2, sums)
+    )(listed, pair_cs, g2, e2, sums)
     mask_grad, resist = pl.pallas_call(
         last_kernel,
         out_shape=(

time: 63.9 us -> 62.2 us (0.973)
  Pallas kernels: 63.1 us -> 61.4 us
    pallas_call x1, Pallas kernels: 55.2 us -> 53.7 us  [local(): pl.pallas_call(main_kernel, out_shape=(jax.ShapeDtypeStruct((2, R, N), BF...]
where the time goes in v5:
time: 62.2 us; the launch traced here: 62 us
  Pallas kernels  61.4 us (99%)
  between operations  0.66 us (1%)
    pallas_call x1, Pallas kernels, local(): pl.pallas_call(main_kernel, out_shape=(jax.ShapeDtypeStruct((2, R, N), BF...  53.7 us
    pallas_call x1, Pallas kernels, local(): pl.pallas_call(rows_kernel, out_shape=jax.ShapeDtypeStruct((T, 2 * Q, 2 *...  6.12 us
    pallas_call x1, Pallas kernels, local(): pl.pallas_call(last_kernel, out_shape=(jax.ShapeDtypeStruct((2, R, N), F3...  1.33 us

profile of v5, /device:TPU:1, one launch (start us, length us, event | category | flops | bytes accessed | tf_op | source)
XLA Modules:
  0.0 62.0 jit_solution(6268142141915520739)
XLA Ops:
  0.6 53.7 %main.1 = (bf16[2,128,512]{2,1,0:T(8,128)(2,1)S(1)}, bf16[128,16,128]{2,1,0:T(8,128)(2,1)S(1)}, f32[128,2,128]{2,1,0:T(2,128)S(1)}, s32[128,1,128]{2,1,0:T(1,128...) custom-call(bf16[2,128,512]{2,1,0:T(8,128)(2,1)} %masks_h.1, ...), custom_call_target="tpu_custom_call" | custom-call | tf_op jit(solution)/shard_map/main/pallas_call | solution.py:641
  54.3 0.2 several.1.sums
  54.6 6.1 %rows.1 = bf16[4,32,128]{2,1,0:T(8,128)(2,1)S(1)} custom-call(s32[8,128]{1,0:T(8,128)S(1)} %get-tuple-element.12.list_v, f32[128,16,128]{2,1,0:T(8,128)S(1)} %get-tuple-element.13.pair_cs, bf16[128,16,128]{2,1,0:T(8,128)(2,1)S(1)} %get-tuple-element.14.g2, f32[128,2,128]{2,1,0:T(2,128)S(1)} %get-tuple-element.15.e2, f32[4,16,128]{2,1,0:T(8,128)S(1)} %several.1.sums), custom_call_target="tpu_custom_call" | custom-call | tf_op jit(solution)/shard_map/rows/pallas_call | solution.py:715
  60.7 1.3 %last.1 = (f32[2,128,512]{2,1,0:T(8,128)}, bf16[2,128,512]{2,1,0:T(8,128)(2,1)}) custom-call(bf16[4,32,128]{2,1,0:T(8,128)(2,1)S(1)} %rows.1, bf16[128,128]{1,0:T(8,128)(2,1)S(1)} %get-tuple-element.17.p_st, bf16[128,512]{1,0:T(8,128)(2,1)S(1)} %get-tuple-element.18.q_st, bf16[2,128,512]{2,1,0:T(8,128)(2,1)S(1)} %get-tuple-element.19.resist_v), custom_call_target="tpu_custom_call" | custom-call | tf_op jit(solution)/shard_map/last/pallas_call | solution.py:726

commit v6 on v5

--- a/solution.py
+++ b/solution.py
@@ -212,9 +212,25 @@
     return rows.astype(jnp.int32)
 
 
+def single_phases(ids, me, rates):
+    row, lane = grid((CTX, 128))
+    match = jnp.where((ids >> 1 == me) & (lane < PAIRS), 1.0, 0.0)
+
+    def column(values):
+        return jnp.broadcast_to(jnp.sum(match * values.astype(F32), axis=1, keepdims=True), (CTX, 128))
+
+    r = column(pltpu.roll(ids, 128 - 32, 1))
+    s = column(pltpu.roll(ids, 128 - 64, 1))
+    second = column(jnp.where(lane >= SRC, 1.0, 0.0))
+    master = column(ids & 1)
+    single = jnp.where(column(jnp.ones_like(match)) == 1.0, 1.0, 0.0)
+    cs = cos_sin([jnp.broadcast_to(rate[H : H + 1], (CTX, 128)) for rate in rates], r, s)
+    return jnp.where(single * (1.0 - master) > 0.5, cs, 0.0), jnp.where(single * master > 0.5, cs, 0.0), single * second
+
+
 def main_kernel(
     masks_h, br_h, bc_h, pupils_h, targets_h, ids_h, shifts_h, fst_h, gcat_h, inv_h, adj_h,
-    resist, g2, e2, ids_all, listed, pair_cs, p_out, q_out,
+    resist, g2, e2, ids_all, listed, pair_cs, single_cs, p_out, q_out,
     masks, br, bc, pupils, targets, fst, gown_v, inv, adj,
     ids_s, shifts_s, list_s, g1, e1, part, part_in, spec, prr, pii, u_all, pull, phases,
     load_sem, list_sem, x_send, x_recv, g_send, a_recv, f_recv, s_send, s_recv, i_send, i_recv, e_send, e_recv,
@@ -330,9 +346,9 @@
 
         for k in NEAR_FIRST:
             along_minor(k, minor_ids[k]).start()
+        between()
         for k in NEAR_FIRST:
             along_major(0, k).start()
-        between()
 
         def forward(i, _):
             came = near_first(i)
@@ -519,12 +535,15 @@
         put(1, c, half_rows, e)
 
     copies = tile_scatter(1)
+    for i, value in enumerate(single_phases(ids_all[...].reshape(CTX, 128), q, rates)):
+        single_cs[i] = value
+    plain_rates = [rate[:H] for rate in rates]
     list_copy.wait()
 
     def pair_phases(i, _):
         for b in range(8):
             k = i * 8 + b
-            pair_cs[k] = cos_sin(rates, list_s[1, k].astype(F32), list_s[2, k].astype(F32))
+            pair_cs[k] = cos_sin(plain_rates, list_s[1, k].astype(F32), list_s[2, k].astype(F32))
         return 0
 
     lax.fori_loop(0, CTX // 8, pair_phases, 0)
@@ -576,7 +595,7 @@
         lax.fori_loop(0, CTX, host, 0)
 
 
-def rows_kernel(list_v, pair_cs, g2, e2, sums, rows, list_s, sem, x_send, x_recv):
+def rows_kernel(list_v, pair_cs, single_cs, g2, e2, sums, rows, list_s, sem, x_send, x_recv):
     tile = lax.axis_index("tile")
     copy = pltpu.make_async_copy(list_v, list_s, sem)
     copy.start()
@@ -585,22 +604,33 @@
         pl.semaphore_signal(barrier, inc=1, device_id={"tile": (tile + k) % T}, device_id_type=MESH)
     left = left_half((Q, 2 * M))
     copy.wait()
-    block = 8
+    block = 16
 
     def step(i, carry):
         total = list(carry)
         for b in range(block):
             k = i * block + b
-            a, b = pair_terms(g2, e2, list_s[0, k], pair_cs[k])
+            context = list_s[0, k]
+            both = g2[context // 2].astype(F32)
+            g = jnp.where(context % 2 > 0, both[H:], both[:H])
+            cs = pair_cs[k]
+            a = g * cs
+            b = swap(g) * cs
             for m in range(2):
                 weight = list_s[3 + m, k].astype(F32)
                 total[2 * m] += a * weight
                 total[2 * m + 1] += b * weight
         return tuple(total)
 
-    total = lax.fori_loop(0, CTX // block, step, tuple(sums[i] for i in range(4)))
+    e = jnp.where(single_cs[2] > 0.5, e2[:, 1, :], e2[:, 0, :])
+    e_turned = swap(e)
+    total = lax.fori_loop(0, CTX // block, step, (jnp.zeros((H, 2 * M), F32),) * 4)
     for m in range(2):
-        a, b = total[2 * m : 2 * m + 2]
+        cs = single_cs[m]
+        a = jnp.sum(e * cs, axis=0, keepdims=True)
+        b = jnp.sum(e_turned * cs, axis=0, keepdims=True)
+        a = sums[2 * m] + jnp.concatenate([total[2 * m], padded(a)], 0)
+        b = sums[2 * m + 1] + jnp.concatenate([total[2 * m + 1], padded(b)], 0)
         rows[tile, m * Q : (m + 1) * Q] = jnp.where(left, a - swap(a), b + swap(b)).astype(BF16)
     pl.semaphore_wait(barrier, T - 1)
     copies = []
@@ -619,7 +649,7 @@
 
 def last_kernel(rows, p_st, q_st, resist_v, out, resist, held, sem):
     left = left_half((M, 2 * M))
-    copies = [pltpu.make_async_copy(resist_v, resist, sem.at[2])]
+    copies = [pltpu.make_async_copy(resist_v, resist, sem.at[4])]
     copies[0].start()
     for m in range(2):
         parts = [rows[t].astype(F32)[m * Q : (m + 1) * Q] for t in range(T)]
@@ -627,9 +657,12 @@
         turned = swap(g)
         both = jnp.concatenate([g, jnp.where(left, turned, -turned)], 0).astype(BF16)
         lifted = dot(p_st[...], both, ((0,), (0,))).astype(BF16)
-        held[m] = dot(lifted, q_st[...])
-        copies.append(pltpu.make_async_copy(held.at[m], out.at[m], sem.at[m]))
-        copies[-1].start()
+        for i in range(2):
+            part = slice(i * (R // 2), (i + 1) * (R // 2))
+            held[m, part] = dot(lifted[part], q_st[...])
+            place = (m, pl.ds(i * (R // 2), R // 2))
+            copies.append(pltpu.make_async_copy(held.at[place], out.at[place], sem.at[2 * m + i]))
+            copies[-1].start()
     wait_all(copies)
 
 
@@ -638,7 +671,7 @@
     hbm = pl.BlockSpec(memory_space=pltpu.HBM)
     dma = pltpu.SemaphoreType.DMA
     stay = functools.partial(pltpu.with_memory_space_constraint, memory_space=pltpu.HBM)
-    resist_v, g2, e2, ids_all, listed, pair_cs, p_st, q_st = pl.pallas_call(
+    resist_v, g2, e2, ids_all, listed, pair_cs, single_cs, p_st, q_st = pl.pallas_call(
         main_kernel,
         out_shape=(
             jax.ShapeDtypeStruct((2, R, N), BF16),
@@ -646,12 +679,13 @@
             jax.ShapeDtypeStruct((CTX, 2, 2 * M), F32),
             jax.ShapeDtypeStruct((CTX, 1, 128), jnp.int32),
             jax.ShapeDtypeStruct((8, 128), jnp.int32),
-            jax.ShapeDtypeStruct((CTX, Q, 2 * M), F32),
+            jax.ShapeDtypeStruct((CTX, H, 2 * M), F32),
+            jax.ShapeDtypeStruct((3, CTX, 2 * M), F32),
             jax.ShapeDtypeStruct((2 * M, R), BF16),
             jax.ShapeDtypeStruct((2 * M, N), BF16),
         ),
         in_specs=[hbm] * 11,
-        out_specs=(vmem,) * 8,
+        out_specs=(vmem,) * 9,
         scratch_shapes=[
             pltpu.VMEM((2, R, N), BF16),
             pltpu.VMEM((N, R), BF16),
@@ -715,14 +749,14 @@
     rows = pl.pallas_call(
         rows_kernel,
         out_shape=jax.ShapeDtypeStruct((T, 2 * Q, 2 * M), BF16),
-        in_specs=[vmem] * 5,
+        in_specs=[vmem] * 6,
         out_specs=vmem,
         scratch_shapes=[pltpu.SMEM((8, 128), jnp.int32), dma, dma((T - 1,)), dma((T - 1,))],
         compiler_params=pltpu.CompilerParams(
             collective_id=1, has_side_effects=True, vmem_limit_bytes=32 << 20
         ),
         name="rows",
-    )(listed, pair_cs, g2, e2, sums)
+    )(listed, pair_cs, single_cs, g2, e2, sums)
     mask_grad, resist = pl.pallas_call(
         last_kernel,
         out_shape=(
@@ -731,7 +765,7 @@
         ),
         in_specs=[vmem] * 4,
         out_specs=(hbm, hbm),
-        scratch_shapes=[pltpu.VMEM((2, R, N), F32), dma((3,))],
+        scratch_shapes=[pltpu.VMEM((2, R, N), F32), dma((5,))],
         compiler_params=pltpu.CompilerParams(vmem_limit_bytes=32 << 20),
         name="last",
     )(rows, p_st, q_st, resist_v)

time: 62.2 us -> 61.4 us (0.987)
  Pallas kernels: 61.4 us -> 60.6 us
    pallas_call x1, Pallas kernels: 6.12 us -> 5.27 us  [local(): pl.pallas_call(rows_kernel, out_shape=jax.ShapeDtypeStruct((T, 2 * Q, 2 *...]
where the time goes in v6:
time: 61.4 us; the launch traced here: 61.3 us
  Pallas kernels  60.6 us (99%)
  between operations  0.66 us (1%)
    pallas_call x1, Pallas kernels, local(): pl.pallas_call(main_kernel, out_shape=(jax.ShapeDtypeStruct((2, R, N), BF...  53.8 us
    pallas_call x1, Pallas kernels, local(): pl.pallas_call(rows_kernel, out_shape=jax.ShapeDtypeStruct((T, 2 * Q, 2 *...  5.27 us
    pallas_call x1, Pallas kernels, local(): pl.pallas_call(last_kernel, out_shape=(jax.ShapeDtypeStruct((2, R, N), F3...  1.33 us

profile of v6, /device:TPU:1, one launch (start us, length us, event | category | flops | bytes accessed | tf_op | source)
XLA Modules:
  0.0 61.3 jit_solution(10141198755226734889)
XLA Ops:
  0.6 53.8 %main.1 = (bf16[2,128,512]{2,1,0:T(8,128)(2,1)S(1)}, bf16[128,16,128]{2,1,0:T(8,128)(2,1)S(1)}, f32[128,2,128]{2,1,0:T(2,128)S(1)}, s32[128,1,128]{2,1,0:T(1,128...) custom-call(bf16[2,128,512]{2,1,0:T(8,128)(2,1)} %masks_h.1, ...), custom_call_target="tpu_custom_call" | custom-call | tf_op jit(solution)/shard_map/main/pallas_call | solution.py:674
  54.4 0.2 several.1.sums
  54.6 5.3 %rows.1 = bf16[4,32,128]{2,1,0:T(8,128)(2,1)S(1)} custom-call(s32[8,128]{1,0:T(8,128)S(1)} %get-tuple-element.13.list_v, f32[128,8,128]{2,1,0:T(8,128)S(1)} %get-tuple-element.14.pair_cs, f32[3,128,128]{2,1,0:T(8,128)S(1)} %get-tuple-element.15.single_cs, bf16[128,16,128]{2,1,0:T(8,128)(2,1)S(1)} %get-tuple-element.16.g2, ...), custom_call_target="tpu_custom_call" | custom-call | tf_op jit(solution)/shard_map/rows/pallas_call | solution.py:749
  59.9 1.3 %last.1 = (f32[2,128,512]{2,1,0:T(8,128)}, bf16[2,128,512]{2,1,0:T(8,128)(2,1)}) custom-call(bf16[4,32,128]{2,1,0:T(8,128)(2,1)S(1)} %rows.1, bf16[128,128]{1,0:T(8,128)(2,1)S(1)} %get-tuple-element.19.p_st, bf16[128,512]{1,0:T(8,128)(2,1)S(1)} %get-tuple-element.20.q_st, bf16[2,128,512]{2,1,0:T(8,128)(2,1)S(1)} %get-tuple-element.21.resist_v), custom_call_target="tpu_custom_call" | custom-call | tf_op jit(solution)/shard_map/last/pallas_call | solution.py:760

commit v7 on v6

--- a/solution.py
+++ b/solution.py
@@ -16,6 +16,7 @@
 M = 64
 K = 6
 T = 4
+FAR_FIRST = (2, 1, 3)
 R = N // T
 H = M // (2 * T)
 Q = 16
@@ -275,7 +276,7 @@
     for k in range(1, SIDE):
         pl.semaphore_signal(barrier, inc=1, device_id={"ctx": ctx_id(major, (minor + k) % SIDE)}, device_id_type=MESH)
         pl.semaphore_signal(barrier, inc=1, device_id={"ctx": ctx_id((major + k) % SIDE, minor)}, device_id_type=MESH)
-    for k in range(1, T):
+    for k in FAR_FIRST:
         pl.semaphore_signal(barrier, inc=1, device_id={"tile": (tile + k) % T}, device_id_type=MESH)
     pl.semaphore_signal(barrier, inc=1, device_id={"ctx": sibling}, device_id_type=MESH)
 
@@ -304,7 +305,7 @@
 
     def tile_scatter(step):
         copies = []
-        for k in range(1, T):
+        for k in FAR_FIRST:
             to = (tile + k) % T
             copies.append(
                 pltpu.make_async_remote_copy(
@@ -457,7 +458,7 @@
             sum_b += swap(g) * cs
         spec[tile, c * Q : (c + 1) * Q] = jnp.where(leftq, sum_a + swap(sum_a), swap(sum_b) - sum_b)
     copies = []
-    for k in range(1, T):
+    for k in FAR_FIRST:
         copies.append(
             pltpu.make_async_remote_copy(
                 src_ref=spec.at[tile], dst_ref=spec.at[tile],
@@ -600,7 +601,7 @@
     copy = pltpu.make_async_copy(list_v, list_s, sem)
     copy.start()
     barrier = pltpu.get_barrier_semaphore()
-    for k in range(1, T):
+    for k in FAR_FIRST:
         pl.semaphore_signal(barrier, inc=1, device_id={"tile": (tile + k) % T}, device_id_type=MESH)
     left = left_half((Q, 2 * M))
     copy.wait()
@@ -634,7 +635,7 @@
         rows[tile, m * Q : (m + 1) * Q] = jnp.where(left, a - swap(a), b + swap(b)).astype(BF16)
     pl.semaphore_wait(barrier, T - 1)
     copies = []
-    for k in range(1, T):
+    for k in FAR_FIRST:
         copies.append(
             pltpu.make_async_remote_copy(
                 src_ref=rows.at[tile], dst_ref=rows.at[tile],

time: 61.4 us -> 61 us (level)
  no operation moved by 1% of the time
where the time goes in v7:
time: 61 us; the launch traced here: 60.9 us
  Pallas kernels  60.2 us (99%)
  between operations  0.66 us (1%)
    pallas_call x1, Pallas kernels, local(): pl.pallas_call(main_kernel, out_shape=(jax.ShapeDtypeStruct((2, R, N), BF...  53.4 us
    pallas_call x1, Pallas kernels, local(): pl.pallas_call(rows_kernel, out_shape=jax.ShapeDtypeStruct((T, 2 * Q, 2 *...  5.25 us
    pallas_call x1, Pallas kernels, local(): pl.pallas_call(last_kernel, out_shape=(jax.ShapeDtypeStruct((2, R, N), F3...  1.33 us

profile of v7, /device:TPU:1, one launch (start us, length us, event | category | flops | bytes accessed | tf_op | source)
XLA Modules:
  0.0 60.9 jit_solution(9848057446003673109)
XLA Ops:
  0.6 53.4 %main.1 = (bf16[2,128,512]{2,1,0:T(8,128)(2,1)S(1)}, bf16[128,16,128]{2,1,0:T(8,128)(2,1)S(1)}, f32[128,2,128]{2,1,0:T(2,128)S(1)}, s32[128,1,128]{2,1,0:T(1,128...) custom-call(bf16[2,128,512]{2,1,0:T(8,128)(2,1)} %masks_h.1, ...), custom_call_target="tpu_custom_call" | custom-call | tf_op jit(solution)/shard_map/main/pallas_call | solution.py:675
  54.1 0.2 several.1.sums
  54.3 5.3 %rows.1 = bf16[4,32,128]{2,1,0:T(8,128)(2,1)S(1)} custom-call(s32[8,128]{1,0:T(8,128)S(1)} %get-tuple-element.13.list_v, f32[128,8,128]{2,1,0:T(8,128)S(1)} %get-tuple-element.14.pair_cs, f32[3,128,128]{2,1,0:T(8,128)S(1)} %get-tuple-element.15.single_cs, bf16[128,16,128]{2,1,0:T(8,128)(2,1)S(1)} %get-tuple-element.16.g2, ...), custom_call_target="tpu_custom_call" | custom-call | tf_op jit(solution)/shard_map/rows/pallas_call | solution.py:750
  59.5 1.3 %last.1 = (f32[2,128,512]{2,1,0:T(8,128)}, bf16[2,128,512]{2,1,0:T(8,128)(2,1)}) custom-call(bf16[4,32,128]{2,1,0:T(8,128)(2,1)S(1)} %rows.1, bf16[128,128]{1,0:T(8,128)(2,1)S(1)} %get-tuple-element.19.p_st, bf16[128,512]{1,0:T(8,128)(2,1)S(1)} %get-tuple-element.20.q_st, bf16[2,128,512]{2,1,0:T(8,128)(2,1)S(1)} %get-tuple-element.21.resist_v), custom_call_target="tpu_custom_call" | custom-call | tf_op jit(solution)/shard_map/last/pallas_call | solution.py:761
